TPU v7x, 256 devices: a whole 4x4x8 slice. The times are simulated.
256 devices in a mesh: lon: 32 (over z, y_hi, core), lat: 8 (over y_lo, x).
Axes of the slice: x: 4, y: 4 (y_hi: 2, y_lo: 2; y = y_hi * 2 + y_lo), z: 8, core: 2. Of those that a mesh axis runs over, the one named last changes fastest.
Arguments:
- hidden_in: bfloat16 [128, 2048, 384], P('lat', 'lon'), may hold values from -6 to 6
- cotangent: bfloat16 [128, 2048, 384], P('lat', 'lon'), may hold values from -6 to 6
- weight_fine: bfloat16 [3, 3, 384, 384], replicated, may hold values from -0.109375 to 0.109375
- weight_mid: bfloat16 [3, 3, 384, 384], replicated, may hold values from -0.109375 to 0.109375
- weight_coarse: bfloat16 [3, 3, 384, 384], replicated, may hold values from -0.109375 to 0.109375
Outputs:
- output: bfloat16 [128, 2048, 384], P('lat', 'lon')
- grad_in: bfloat16 [128, 2048, 384], P('lat', 'lon')
All inputs are finite; a program needn't handle non-finite values.
Results may differ from a plain program's by a relative error of at most 0.012.
Values may be sent and summed in bfloat16 or wider, within the bound.
A program may use at most 64 MiB of HBM per device.

v0:
```python
import functools

import jax
import jax.numpy as jnp
from jax import lax
from jax.experimental import pallas as pl
from jax.experimental.pallas import tpu as pltpu
from jax.sharding import PartitionSpec as P

MESH = pl.DeviceIdType.MESH
F32 = jnp.float32
BF16 = jnp.bfloat16
C = 384
LANES = 3


def get(ref, start, n, stride=1):
    ds = pl.ds(start, n) if stride == 1 else pl.ds(start, n, stride=stride)
    return jnp.concatenate([ref[l, ds, :] for l in range(LANES)], axis=-1)


def put(ref, start, val, stride=1):
    n = val.shape[0]
    ds = pl.ds(start, n) if stride == 1 else pl.ds(start, n, stride=stride)
    for l in range(LANES):
        ref[l, ds, :] = val[:, l * 128 : (l + 1) * 128]


class Rows:
    def __init__(self, ref, pitch):
        self.ref, self.pitch = ref, pitch


def at_row(grid, r, start):
    if isinstance(r, int):
        return r * grid.pitch + start
    if start % 8 == 0 and grid.pitch % 8 == 0:
        return pl.multiple_of(r * grid.pitch + start, 8)
    return r * grid.pitch + start


def row_get(grid, r, start, n, stride=1):
    return get(grid.ref, at_row(grid, r, start), n, stride)


def row_put(grid, r, start, val, stride=1):
    put(grid.ref, at_row(grid, r, start), val, stride)


def col_get(grid, c, r0, n):
    return get(grid.ref, r0 * grid.pitch + c, n, grid.pitch)


def col_put(grid, c, r0, val):
    put(grid.ref, r0 * grid.pitch + c, val, grid.pitch)


def gelu_pair(z):
    e = jnp.exp(-0.5 * z * z)
    t = 1.0 / (1.0 + (0.3275911 * 0.7071067811865476) * jnp.abs(z))
    q = t * (
        0.127414796
        + t * (-0.142248368 + t * (0.7107068705 + t * (-0.7265760135 + t * 0.5307027145)))
    )
    h = q * e
    cdf = jnp.where(z >= 0, 1.0 - h, h)
    return z * cdf, cdf + z * (e * 0.3989422804014327)


def rounded(x):
    return x.astype(BF16).astype(F32)


def conv_dot(parts, weight):
    lhs = jnp.concatenate([parts(a, b) for a in range(3) for b in range(3)], axis=-1)
    return jnp.dot(lhs, weight[...].reshape(9 * C, C), preferred_element_type=F32)


def conv_dot_t(parts, weight):
    lhs = jnp.concatenate([parts(a, b) for a in range(3) for b in range(3)], axis=-1)
    rhs = jnp.concatenate([weight[a, b] for a in range(3) for b in range(3)], axis=-1)
    return lax.dot_general(lhs, rhs, (((1,), (1,)), ((), ())), preferred_element_type=F32)


def kernel(
    nlat, nlon,
    hid_hbm, cot_hbm, wf_hbm, wm_hbm, wc_hbm, out_hbm, grad_hbm,
    hid, cot, wf, wm, wc, out_v, grad_v,
    s_ext, e_ext, l_edge, pre, pre_e, act, slp, act_e, slp_e,
    sx, ctp, cte, gma, gmae, gcax,
    pf, sm0, sm1, pre_m, am, slm, sle, slb, pml, sc, cb, ac, gs, gb, bm,
    mg, ms0, ms1, mc, ml, bfm, bfe, g_ext, fs0, fs3, ge, ns, tile, ts,
    c_buf, k_buf, r_slot, c_slot, k_slot,
    lr_buf, lc_buf, lr_slot, lc_slot,
    pc_buf, pr_slot, sr_slot, pc_slot,
    lsem, ssem, rsem,
):
    s_ext = Rows(s_ext, 80)
    act = Rows(act, 64)
    slp = Rows(slp, 64)
    act_e = Rows(act_e, 40)
    slp_e = Rows(slp_e, 32)
    sx = Rows(sx, 64)
    cte = Rows(cte, 32)
    gma = Rows(gma, 32)
    gmae = Rows(gmae, 16)
    gcax = Rows(gcax, 32)
    sm0 = Rows(sm0, 32)
    sm1 = Rows(sm1, 32)
    slm = Rows(slm, 32)
    sle = Rows(sle, 16)
    sc = Rows(sc, 48)
    gs = Rows(gs, 48)
    bm = Rows(bm, 32)
    ms0 = Rows(ms0, 32)
    ms1 = Rows(ms1, 32)
    mc = Rows(mc, 24)
    bfe = Rows(bfe, 16)
    fs0 = Rows(fs0, 32)
    fs3 = Rows(fs3, 32)
    ge = Rows(ge, 32)
    ns = Rows(ns, 64)
    lat = lax.axis_index("lat")
    lon = lax.axis_index("lon")
    north = lat == 0
    south = lat == nlat - 1
    sgn_n = jnp.where(north, -1, 1)
    sgn_s = jnp.where(south, -1, 1)

    def device(dlat, dlon):
        to_lat, to_lon = lat, lon + dlon + nlon
        if dlat:
            pole = north if dlat < 0 else south
            to_lat = jnp.where(pole, lat, lat + dlat)
            to_lon = to_lon + jnp.where(pole, nlon // 2, 0)
        return {"lat": to_lat, "lon": lax.rem(to_lon, nlon)}

    there = [device(*d) for d in ((-1, 0), (1, 0), (0, -1), (0, 1), (-1, -1), (-1, 1), (1, -1), (1, 1))]
    slot = [
        jnp.where(north, 0, 1), jnp.where(south, 1, 0), 3, 2,
        jnp.where(north, 5, 7), jnp.where(north, 4, 6),
        jnp.where(south, 7, 5), jnp.where(south, 6, 4),
    ]

    def remote(kind, d, src, dst, where):
        return pltpu.make_async_remote_copy(
            src_ref=src, dst_ref=dst, send_sem=ssem.at[kind, d], recv_sem=rsem.at[kind, where],
            device_id=there[d], device_id_type=MESH,
        )

    def load(i, src, dst):
        copy = pltpu.make_async_copy(src, dst, lsem.at[i])
        copy.start()
        return copy

    barrier = pltpu.get_barrier_semaphore()
    for t in there:
        pl.semaphore_signal(barrier, inc=1, device_id=t, device_id_type=MESH)

    hid_in = load(0, hid_hbm, hid)
    wf_in = load(1, wf_hbm, wf)
    cot_in = load(2, cot_hbm, cot)
    wm_in = load(3, wm_hbm, wm)
    wc_in = load(4, wc_hbm, wc)
    hid_in.wait()

    @pl.loop(0, 16)
    def _(r):
        row_put(s_ext, r + 3, 8, hid[r].astype(F32))

    for side, first in ((0, 0), (1, 61)):
        for c in range(3):
            c_buf[side, pl.ds(c * 16, 16)] = col_get(s_ext, 8 + first + c, 3, 16).astype(BF16)
    for k, (row, first) in enumerate(((0, 0), (0, 61), (12, 0), (12, 61))):
        for c in range(3):
            put(tile, c * 4, col_get(s_ext, 8 + first + c, 3 + row, 8)[:4])
        k_buf[k] = get(tile, 0, 16).astype(BF16)

    pl.semaphore_wait(barrier, 8)

    sends = []

    def send(kind, d, src, slots, base):
        copy = remote(kind, d, src, slots.at[slot[d] - base], slot[d])
        copy.start()
        sends.append(copy)

    def recv(kind, where, src, dst):
        remote(kind, where, src, dst, where).wait_recv()

    send(0, 0, hid.at[pl.ds(0, 3)], r_slot, 0)
    send(0, 1, hid.at[pl.ds(13, 3)], r_slot, 0)
    for d in (4, 5, 6, 7):
        send(0, d, k_buf.at[d - 4], k_slot, 4)
    for d in (2, 3):
        send(0, d, c_buf.at[d - 2], c_slot, 2)

    @pl.loop(0, 16)
    def _(r):
        for ph in range(6):
            e_ext[r + 3, ph] = row_get(s_ext, r + 3, 7 + ph, 16, 4).astype(BF16)

    wf_in.wait()
    pre[pl.ds(3, 14)] = conv_dot(
        lambda a, b: e_ext[3 + a : 17 + a, b : b + 4].reshape(14 * 64, C), wf
    ).reshape(14, 64, C)

    def fine_gelu(i):
        a, s = gelu_pair(pre[i])
        row_put(act, i, 0, rounded(a))
        row_put(slp, i, 0, s)

    @pl.loop(3, 17)
    def _(i):
        fine_gelu(i)

    cot_in.wait()

    @pl.loop(0, 16)
    def _(r):
        row_put(sx, r, 0, cot[r].astype(F32))
        for p in range(4):
            ctp[r + 1, pl.ds(p * 16, 16)] = row_get(sx, r, p, 16, 4).astype(BF16)

    @pl.loop(0, 8)
    def _(m):
        for p in range(2):
            total = 0.0
            for dr in range(2):
                for dp in range(2):
                    total = total + ctp[2 * m + dr + 1, pl.ds((2 * p + dp) * 16, 16)].astype(F32)
            row_put(gma, m + 2, p * 16, total)

    for q in range(4):
        total = 0.0
        for dr in range(2):
            for p in range(2):
                total = total + row_get(gma, 2 * q + dr + 2, p * 16, 16)
        row_put(gcax, q + 2, 8, total)

    for side, (row, mid, coarse) in enumerate(((0, 0, 0), (15, 6, 2))):
        lr_buf[side, pl.ds(0, 64)] = ctp[row + 1]
        for k in range(2):
            lr_buf[side, pl.ds(64 + 32 * k, 32)] = row_get(gma, mid + k + 2, 0, 32).astype(BF16)
            lr_buf[side, pl.ds(128 + 16 * k, 16)] = row_get(gcax, coarse + k + 2, 8, 16).astype(BF16)
    for side, (col, mids, coarse) in enumerate(((0, (0, 16), 0), (63, (15, 31), 14))):
        put(tile, 0, col_get(sx, col, 0, 16))
        for c in range(2):
            put(tile, 16 + 8 * c, col_get(gma, mids[c], 2, 8))
            put(tile, 32 + 4 * c, col_get(gcax, 8 + coarse + c, 2, 8)[:4])
        lc_buf[side] = get(tile, 0, 48).astype(BF16)
    for d in (0, 1):
        send(1, d, lr_buf.at[d], lr_slot, 0)
    for d in range(2, 8):
        send(1, d, lc_buf.at[d % 2], lc_slot, 2)

    for k in range(2):
        recv(0, k, hid.at[pl.ds(0, 3)], r_slot.at[k])
    for k in range(4):
        recv(0, 4 + k, k_buf.at[k], k_slot.at[k])
    for k in range(2):
        recv(0, 2 + k, c_buf.at[k], c_slot.at[k])

    for j in range(3):
        row_put(s_ext, 2 - j, 8, r_slot[0, jnp.where(north, j, 2 - j)].astype(F32))
        row_put(s_ext, 19 + j, 8, r_slot[1, jnp.where(south, 2 - j, j)].astype(F32))
    for side, first in ((0, -3), (1, 64)):
        for c in range(3):
            col_put(s_ext, 8 + first + c, 3, c_slot[side, pl.ds(c * 16, 16)].astype(F32))
    for k in range(4):
        put(tile, 0, k_slot[k].astype(F32))
        first = 64 if k % 2 else -3
        for c in range(3):
            for j in range(3):
                if k < 2:
                    at, row = jnp.where(north, j, 3 - j), 2 - j
                else:
                    at, row = jnp.where(south, 3 - j, j), 19 + j
                row_put(s_ext, row, 8 + first + c, get(tile, c * 4 + at, 1))

    @pl.loop(0, 6)
    def _(i):
        r = i + jnp.where(i >= 3, 16, 0)
        for ph in range(6):
            e_ext[r, ph] = row_get(s_ext, r, 7 + ph, 16, 4).astype(BF16)

    for r in (3, 4, 17, 18):
        for ph in (0, 5):
            e_ext[r, ph] = row_get(s_ext, r, 7 + ph, 16, 4).astype(BF16)

    edge_rows = lax.broadcasted_iota(jnp.int32, (32, 1), 0)
    flip = (north & (edge_rows < 2)) | (south & ((edge_rows == 18) | (edge_rows == 19)))

    @pl.loop(0, 10)
    def _(i):
        side = i // 5
        col = 8 - 3 + i + side * 60
        low, mid, high = (get(s_ext.ref, a * 80 + col, 32, 80) for a in range(3))
        l_edge[0, i] = jnp.where(flip, high, low).astype(BF16)
        l_edge[1, i] = mid.astype(BF16)
        l_edge[2, i] = jnp.where(flip, low, high).astype(BF16)

    def ring(a, b):
        rows = [1 + sgn_n * (a - 1), 2 + sgn_n * (a - 1), 2 + a, 17 + a, 19 + sgn_s * (a - 1), 20 + sgn_s * (a - 1)]
        parts = [e_ext[r, b : b + 4].reshape(64, C) for r in rows]
        parts += [l_edge[a, s * 5 + b : s * 5 + b + 3].reshape(96, C) for s in range(2)]
        return jnp.concatenate(parts, axis=0)

    res = conv_dot(ring, wf)
    for k, i in enumerate((0, 1, 2, 17, 18, 19)):
        pre[i] = res[k * 64 : (k + 1) * 64]
    pre_e[...] = res[384:].reshape(6, 32, C)

    @pl.loop(0, 6)
    def _(i):
        fine_gelu(i + jnp.where(i >= 3, 14, 0))
        a, s = gelu_pair(pre_e[i])
        row_put(act_e, i, 0, rounded(a))
        row_put(slp_e, i, 0, s)

    for dst, src in ((act, act_e), (slp, slp_e)):
        col_put(dst, 0, 0, row_get(src, 2, 0, 24))
        col_put(dst, 63, 0, row_get(src, 3, 0, 24))

    @pl.loop(0, 10)
    def _(m):
        for p, shifted in ((0, sm0), (1, sm1)):
            total = 0.0
            for dr in range(2):
                for dp in range(2):
                    total = total + row_get(act, 2 * m + dr, (2 * p + dp) * 16, 16)
            total = 0.25 * total
            pf[m, 1 + p] = total.astype(BF16)
            row_put(shifted, m, 8, total)

    for first, shifted, at in ((0, sm1, 7), (4, sm0, 24)):
        total = 0.0
        for c in range(2):
            for dr in range(2):
                total = total + row_get(act_e, first + c, dr, 16, 2)
        col_put(shifted, at, 0, 0.25 * total)

    @pl.loop(0, 10)
    def _(m):
        pf[m, 0] = row_get(sm1, m, 7, 16).astype(BF16)
        pf[m, 3] = row_get(sm0, m, 9, 16).astype(BF16)

    wm_in.wait()
    pre_m[...] = conv_dot(
        lambda a, b: pf[a : a + 8, b : b + 2].reshape(256, C), wm
    ).reshape(8, 32, C)

    @pl.loop(0, 8)
    def _(m):
        a, s = gelu_pair(pre_m[m])
        am[m] = rounded(a)
        row_put(slm, m + 2, 0, s)
        slb[m] = s.astype(BF16)

    for q in range(4):
        total = 0.0
        for dr in range(2):
            for p in range(2):
                total = total + am[2 * q + dr, pl.ds(p * 16, 16)]
        total = 0.25 * total
        pml[q] = total.astype(BF16)
        row_put(sc, q + 3, 16, total)
    for side, (first, mids) in enumerate(((0, (0, 16)), (13, (15, 31)))):
        for c in range(3):
            put(tile, c * 4, col_get(sc, 16 + first + c, 3, 8)[:4])
        for c in range(2):
            put(tile, 16 + 8 * c, col_get(slm, mids[c], 2, 8))
        pc_buf[side] = get(tile, 0, 32).astype(BF16)

    for d in (0, 1):
        send(2, d, pml.at[pl.ds(d, 3)], pr_slot, 0)
    for d in (4, 5, 6, 7, 2, 3):
        send(2, d, pc_buf.at[d % 2], pc_slot, 2)
    for d in (0, 1):
        send(3, d, slb.at[pl.ds(6 * d, 2)], sr_slot, 0)

    for k in range(2):
        recv(1, k, lr_buf.at[k], lr_slot.at[k])
    for k in range(6):
        recv(1, 2 + k, lc_buf.at[0], lc_slot.at[k])
    for k in range(6):
        put(ts, k * 48, lc_slot[k].astype(F32))
    ctp[0] = lr_slot[0, pl.ds(0, 64)]
    ctp[17] = lr_slot[1, pl.ds(0, 64)]

    def pick(k, at):
        return get(ts, k * 48 + at, 1)

    def edge_columns(dst, base):
        for side in range(2):
            for c in range(2):
                to = side * 2 + c
                row_put(dst, to, 2, get(ts, side * 48 + base + 8 * c, 8))
                for j in range(2):
                    at = base + 8 * c + jnp.where(north, j, 7 - j)
                    row_put(dst, to, 1 - j, pick(2 + side, at))
                    at = base + 8 * c + jnp.where(south, 7 - j, j)
                    row_put(dst, to, 10 + j, pick(4 + side, at))

    for j in range(2):
        at_n, at_s = jnp.where(north, j, 1 - j), jnp.where(south, 1 - j, j)
        row_put(gma, 1 - j, 0, lr_slot[0, pl.ds(pl.multiple_of(64 + 32 * at_n, 32), 32)].astype(F32))
        row_put(gma, 10 + j, 0, lr_slot[1, pl.ds(pl.multiple_of(64 + 32 * at_s, 32), 32)].astype(F32))
        row_put(gcax, 1 - j, 8, lr_slot[0, pl.ds(pl.multiple_of(128 + 16 * at_n, 16), 16)].astype(F32))
        row_put(gcax, 6 + j, 8, lr_slot[1, pl.ds(pl.multiple_of(128 + 16 * at_s, 16), 16)].astype(F32))
    for side in range(2):
        row_put(cte, side, 2, get(ts, side * 48, 16))
        row_put(cte, side, 1, pick(2 + side, jnp.where(north, 0, 15)))
        row_put(cte, side, 18, pick(4 + side, jnp.where(south, 15, 0)))
        for c in range(2):
            col = 8 + (16 if side else -2) + c
            for q in range(4):
                row_put(gcax, q + 2, col, pick(side, 32 + 4 * c + q))
            for j in range(2):
                row_put(gcax, 1 - j, col, pick(2 + side, 32 + 4 * c + jnp.where(north, j, 3 - j)))
                row_put(gcax, 6 + j, col, pick(4 + side, 32 + 4 * c + jnp.where(south, 3 - j, j)))
    edge_columns(gmae, 16)

    wc_in.wait()
    for k in range(2):
        recv(2, k, pml.at[pl.ds(0, 3)], pr_slot.at[k])
    for k in range(6):
        recv(2, 2 + k, pc_buf.at[0], pc_slot.at[k])
    for k in range(6):
        put(ts, k * 48, pc_slot[k].astype(F32))
    for j in range(3):
        row_put(sc, 2 - j, 16, pr_slot[0, jnp.where(north, j, 2 - j)].astype(F32))
        row_put(sc, 7 + j, 16, pr_slot[1, jnp.where(south, 2 - j, j)].astype(F32))
    for side in range(2):
        for c in range(3):
            col = 16 + (16 if side else -3) + c
            for q in range(4):
                row_put(sc, q + 3, col, pick(side, 4 * c + q))
            for j in range(3):
                row_put(sc, 2 - j, col, pick(2 + side, 4 * c + jnp.where(north, j, 3 - j)))
                row_put(sc, 7 + j, col, pick(4 + side, 4 * c + jnp.where(south, 3 - j, j)))

    @pl.loop(0, 10)
    def _(r):
        for b in range(3):
            cb[b, r] = row_get(sc, r, 7 + b, 32).astype(BF16)

    def coarse(a, b):
        rows = [1 + sgn_n * (a - 1), 2 + sgn_n * (a - 1)]
        tail = [7 + sgn_s * (a - 1), 8 + sgn_s * (a - 1)]
        parts = [cb[b, r] for r in rows] + [cb[b, 2 + a : 6 + a].reshape(128, C)]
        return jnp.concatenate(parts + [cb[b, r] for r in tail], axis=0)

    res = conv_dot(coarse, wc)
    for i in range(8):
        a, s = gelu_pair(res[i * 32 : (i + 1) * 32])
        if 2 <= i < 6:
            ac[i - 2] = rounded(a[8:24])
        row_put(gs, i, 8, row_get(gcax, i, 0, 32) * s)

    @pl.loop(0, 8)
    def _(r):
        for d in range(3):
            gb[d, r] = row_get(gs, r, 7 + d, 32).astype(BF16)

    for d in range(3):
        for k, (x, y) in enumerate(((0, 2), (1, 3), (4, 6), (5, 7))):
            gb[d, 8 + k] = (gb[d, x].astype(F32) + gb[d, y].astype(F32)).astype(BF16)
        gb[d, 12] = jnp.zeros((32, C), BF16)

    def coarse_t(a, b):
        d = 2 - b
        if a == 1:
            return gb[d, 1:7].reshape(192, C)
        if a == 0:
            rows = [jnp.where(north, 8, 2), jnp.where(north, 9, 3), 4, 5, jnp.where(south, 12, 6), jnp.where(south, 12, 7)]
        else:
            rows = [jnp.where(north, 12, 0), jnp.where(north, 12, 1), 2, 3, jnp.where(south, 10, 4), jnp.where(south, 11, 5)]
        return jnp.concatenate([gb[d, r] for r in rows], axis=0)

    res = conv_dot_t(coarse_t, wc)
    for i in range(6):
        row_put(bm, i, 0, 0.25 * res[i * 32 : (i + 1) * 32])

    for k in range(2):
        recv(3, k, slb.at[pl.ds(0, 2)], sr_slot.at[k])
    for j in range(2):
        row_put(slm, 1 - j, 0, sr_slot[0, jnp.where(north, j, 1 - j)].astype(F32))
        row_put(slm, 10 + j, 0, sr_slot[1, jnp.where(south, 1 - j, j)].astype(F32))
    edge_columns(sle, 16)

    @pl.loop(0, 12)
    def _(k):
        below = row_get(bm, k // 2, 8, 16)
        for p, shifted in ((0, ms0), (1, ms1)):
            g = (row_get(gma, k, p * 16, 16) + below) * row_get(slm, k, p * 16, 16)
            mg[k, 1 + p] = g.astype(BF16)
            row_put(shifted, k, 8, g)

    for side in range(2):
        below = col_get(bm, 24 if side else 7, 0, 8)
        put(tile, 0, below, 2)
        put(tile, 1, below, 2)
        below = get(tile, 0, 16)
        for c in range(2):
            g = (row_get(gmae, side * 2 + c, 0, 16) + below) * row_get(sle, side * 2 + c, 0, 16)
            row_put(mc, side * 3 + (c + 1 if side else c), 0, g)
            if side == 0 and c == 1:
                col_put(ms1, 7, 0, g)
            if side == 1 and c == 0:
                col_put(ms0, 24, 0, g)
    row_put(mc, 2, 0, col_get(ms0, 8, 0, 16))
    row_put(mc, 3, 0, col_get(ms1, 23, 0, 16))

    @pl.loop(0, 12)
    def _(k):
        mg[k, 0] = row_get(ms1, k, 7, 16).astype(BF16)
        mg[k, 3] = row_get(ms0, k, 9, 16).astype(BF16)

    for k, (x, y) in enumerate(((0, 2), (1, 3), (8, 10), (9, 11))):
        mg[12 + k] = (mg[x].astype(F32) + mg[y].astype(F32)).astype(BF16)
    mg[16] = jnp.zeros((4, 16, C), BF16)

    half_rows = lax.broadcasted_iota(jnp.int32, (16, 1), 0)
    at_north = north & (half_rows < 2)
    at_south = south & ((half_rows == 8) | (half_rows == 9))
    for i in range(6):
        low, mid, high = (rounded(row_get(mc, i, e, 16)) for e in range(3))
        both = low + high
        ml[0, i] = jnp.where(at_north, both, jnp.where(at_south, 0.0, high)).astype(BF16)
        ml[1, i] = mid.astype(BF16)
        ml[2, i] = jnp.where(at_south, both, jnp.where(at_north, 0.0, low)).astype(BF16)

    def mid_t(a, b):
        ph = slice(2 - b, 4 - b)
        if a == 1:
            parts = [mg[1:11, ph].reshape(320, C)]
        else:
            if a == 0:
                top = [jnp.where(north, 12, 2), jnp.where(north, 13, 3)]
                body, tail = 4, [jnp.where(south, 16, 10), jnp.where(south, 16, 11)]
            else:
                top = [jnp.where(north, 16, 0), jnp.where(north, 16, 1)]
                body, tail = 2, [jnp.where(south, 14, 8), jnp.where(south, 15, 9)]
            parts = [mg[r, ph].reshape(32, C) for r in top]
            parts += [mg[body : body + 6, ph].reshape(192, C)]
            parts += [mg[r, ph].reshape(32, C) for r in tail]
        return jnp.concatenate(parts + [ml[a, 2 - b], ml[a, 5 - b]], axis=0)

    res = 0.25 * conv_dot_t(mid_t, wm)
    bfm[...] = res[:320].reshape(10, 32, C)
    for side in range(2):
        row_put(bfe, side, 0, res[320 + 16 * side : 336 + 16 * side])

    @pl.loop(0, 18)
    def _(k):
        for p in range(4):
            g = (
                ctp[k, pl.ds(p * 16, 16)].astype(F32) + bfm[(k + 1) // 2, pl.ds((p // 2) * 16, 16)]
            ) * row_get(slp, k + 1, p * 16, 16)
            g_ext[k, 1 + p] = g.astype(BF16)
            if p == 0:
                row_put(fs0, k, 8, g)
            if p == 3:
                row_put(fs3, k, 8, g)

    for side, (shifted, at) in enumerate(((fs3, 7), (fs0, 24))):
        below = row_get(bfe, side, 0, 16)
        put(tile, 0, below, 2)
        put(tile, 1, below, 2)
        g = (row_get(cte, side, 0, 32) + get(tile, 0, 32)) * row_get(slp_e, 1 + 3 * side, 0, 32)
        row_put(ge, side, 0, g)
        col_put(shifted, at, 0, row_get(ge, side, 1, 24))

    @pl.loop(0, 18)
    def _(k):
        g_ext[k, 0] = row_get(fs3, k, 7, 16).astype(BF16)
        g_ext[k, 5] = row_get(fs0, k, 9, 16).astype(BF16)

    for k, (x, y) in enumerate(((0, 2), (15, 17))):
        g_ext[18 + k] = (g_ext[x].astype(F32) + g_ext[y].astype(F32)).astype(BF16)
    g_ext[20] = jnp.zeros((6, 16, C), BF16)

    def fine_t(a, b):
        ph = slice(2 - b, 6 - b)
        if a == 1:
            return g_ext[1:17, ph].reshape(1024, C)
        if a == 0:
            top, body, tail = jnp.where(north, 18, 2), 3, jnp.where(south, 20, 17)
        else:
            top, body, tail = jnp.where(north, 20, 0), 1, jnp.where(south, 19, 15)
        parts = [g_ext[top, ph].reshape(64, C), g_ext[body : body + 14, ph].reshape(896, C)]
        return jnp.concatenate(parts + [g_ext[tail, ph].reshape(64, C)], axis=0)

    pre[pl.ds(0, 16)] = conv_dot_t(fine_t, wf).reshape(16, 64, C)

    @pl.loop(0, 16)
    def _(r):
        for p in range(4):
            v = row_get(act, r + 2, p * 16, 16) + (am[r // 2, pl.ds((p // 2) * 16, 16)] + ac[r // 4])
            row_put(ns, r, p, v, 4)
            row_put(sx, r, p, pre[r, pl.ds(p * 16, 16)], 4)
        out_v[r] = row_get(ns, r, 0, 64).astype(BF16)
        grad_v[r] = row_get(sx, r, 0, 64).astype(BF16)

    a = load(5, out_v, out_hbm)
    b = load(6, grad_v, grad_hbm)
    for copy in sends:
        copy.wait_send()
    a.wait()
    b.wait()


def body(nlat, nlon, hidden_in, cotangent, weight_fine, weight_mid, weight_coarse):
    hbm = pl.BlockSpec(memory_space=pl.ANY)
    field = (16, 64, C)
    weight = (3, 3, C, C)

    def v(*shape, dtype=BF16):
        return pltpu.VMEM(shape, dtype)

    def f(*shape):
        return pltpu.VMEM(shape, F32)

    scratch = dict(
        hid=v(*field), cot=v(*field), wf=v(*weight), wm=v(*weight), wc=v(*weight), out_v=v(*field), grad_v=v(*field),
        s_ext=f(3, 36 * 80, 128), e_ext=v(22, 6, 16, C), l_edge=v(3, 10, 32, C), pre=f(24, 64, C), pre_e=f(6, 32, C),
        act=f(3, 24 * 64, 128), slp=f(3, 24 * 64, 128), act_e=f(3, 6 * 40, 128), slp_e=f(3, 6 * 32, 128),
        sx=f(3, 16 * 64, 128), ctp=v(18, 64, C), cte=f(3, 2 * 32, 128), gma=f(3, 16 * 32, 128), gmae=f(3, 4 * 16, 128),
        gcax=f(3, 16 * 32, 128),
        pf=v(10, 4, 16, C), sm0=f(3, 16 * 32, 128), sm1=f(3, 16 * 32, 128), pre_m=f(8, 32, C), am=f(8, 32, C),
        slm=f(3, 16 * 32, 128), sle=f(3, 4 * 16, 128), slb=v(8, 32, C), pml=v(4, 16, C), sc=f(3, 12 * 48, 128),
        cb=v(3, 10, 32, C), ac=f(4, 16, C), gs=f(3, 8 * 48, 128), gb=v(3, 13, 32, C), bm=f(3, 8 * 32, 128),
        mg=v(17, 4, 16, C), ms0=f(3, 16 * 32, 128), ms1=f(3, 16 * 32, 128), mc=f(3, 6 * 24, 128), ml=v(3, 6, 16, C),
        bfm=f(10, 32, C), bfe=f(3, 2 * 16, 128), g_ext=v(21, 6, 16, C), fs0=f(3, 24 * 32, 128), fs3=f(3, 24 * 32, 128),
        ge=f(3, 2 * 32, 128), ns=f(3, 16 * 64, 128), tile=f(3, 48, 128), ts=f(3, 288, 128),
        c_buf=v(2, 48, C), k_buf=v(4, 16, C), r_slot=v(2, 3, 64, C), c_slot=v(2, 48, C), k_slot=v(4, 16, C),
        lr_buf=v(2, 160, C), lc_buf=v(2, 48, C), lr_slot=v(2, 160, C), lc_slot=v(6, 48, C),
        pc_buf=v(2, 32, C), pr_slot=v(2, 3, 16, C), sr_slot=v(2, 2, 32, C), pc_slot=v(6, 32, C),
        lsem=pltpu.SemaphoreType.DMA((8,)), ssem=pltpu.SemaphoreType.DMA((4, 8)), rsem=pltpu.SemaphoreType.DMA((4, 8)),
    )
    shape = jax.ShapeDtypeStruct(field, BF16)
    return pl.pallas_call(
        functools.partial(kernel, nlat, nlon),
        out_shape=(shape, shape),
        in_specs=[hbm] * 5,
        out_specs=(hbm, hbm),
        scratch_shapes=list(scratch.values()),
        compiler_params=pltpu.CompilerParams(
            collective_id=0, has_side_effects=True, vmem_limit_bytes=60 * 2**20
        ),
    )(hidden_in, cotangent, weight_fine, weight_mid, weight_coarse)


def solution(mesh):
    field = P("lat", "lon", None)
    return jax.shard_map(
        functools.partial(body, mesh.shape["lat"], mesh.shape["lon"]),
        mesh=mesh,
        in_specs=(field, field, P(), P(), P()),
        out_specs=(field, field),
        check_vma=False,
    )
```

profile of v0, /device:TPU:1, one launch (start us, length us, event | category | flops | bytes accessed | tf_op | source)
XLA Modules:
  0.0 54.2 jit_solution(13924742325702960093)
XLA Ops:
  0.6 49.4 %shard_map.68 = (bf16[16,64,384]{2,1,0:T(8,128)(2,1)}, bf16[16,64,384]{2,1,0:T(8,128)(2,1)}) custom-call(bf16[16,64,384]{2,1,0:T(8,128)(2,1)} %hid_hbm.1, bf16[16,64,384]{2,1,0:T(8,128)(2,1)} %cot_hbm.1, bf16[3,3,384,384]{3,2,1,0:T(8,128)(2,1)} %wf_hbm.1, bf16[3,3,384,384]{3,2,1,0:T(8,128)(2,1)} %wm_hbm.1, bf16[3,3,384,384]{3,2,1,0:T(8,128)(2,1)} %wc_hbm.1), custom_call_target="tpu_custom_call" | custom-call | tf_op jit(solution)/shard_map/pallas_call | solution.py:643
  50.0 2.1 %copy.9 = bf16[16,64,384]{2,1,0:T(8,128)(2,1)} copy(bf16[16,64,384]{2,1,0:T(8,128)(2,1)} %get-tuple-element.4) | data formatting | bytes 1572864
  52.1 2.1 %copy.10 = bf16[16,64,384]{2,1,0:T(8,128)(2,1)} copy(bf16[16,64,384]{2,1,0:T(8,128)(2,1)} %get-tuple-element.5) | data formatting | bytes 1572864
where the time goes:
time: 54.4 us; the launch traced here: 54.2 us
  Pallas kernels  49.4 us (91%)
  local copies, waits for them, and re-layouts  4.18 us (8%)
  between operations  0.64 us (1%)
    pallas_call x1, Pallas kernels, body(): pl.pallas_call(functools.partial(kernel, nlat, nlon), out_shape=(shape, s...  49.4 us
    unnamed x2, local copies, waits for them, and re-layouts  4.18 us

commit v1 on v0

--- a/solution.py
+++ b/solution.py
@@ -84,15 +84,15 @@
 
 def kernel(
     nlat, nlon,
-    hid_hbm, cot_hbm, wf_hbm, wm_hbm, wc_hbm, out_hbm, grad_hbm,
-    hid, cot, wf, wm, wc, out_v, grad_v,
-    s_ext, e_ext, l_edge, pre, pre_e, act, slp, act_e, slp_e,
+    hid_hbm, cot_hbm, wf_hbm, wm_hbm, wc_hbm, out_v, g_ext, wf,
+    hid, cot, wm, wc,
+    s_ext, e_ext, l_edge, l_late, pre, pre_e, act, slp, act_e, slp_e,
     sx, ctp, cte, gma, gmae, gcax,
     pf, sm0, sm1, pre_m, am, slm, sle, slb, pml, sc, cb, ac, gs, gb, bm,
-    mg, ms0, ms1, mc, ml, bfm, bfe, g_ext, fs0, fs3, ge, ns, tile, ts,
+    mg, ms0, ms1, mc, ml, bfm, bfe, fs0, fs3, ge, ns, tile, ts, tk,
     c_buf, k_buf, r_slot, c_slot, k_slot,
-    lr_buf, lc_buf, lr_slot, lc_slot,
-    pc_buf, pr_slot, sr_slot, pc_slot,
+    lr_buf, lc_buf, lk_buf, lr_slot, lc_slot, lk_slot,
+    pc_buf, pk_buf, pr_slot, sr_slot, ct_slot, pc_slot, pk_slot,
     lsem, ssem, rsem,
 ):
     s_ext = Rows(s_ext, 80)
@@ -159,12 +159,22 @@
 
     hid_in = load(0, hid_hbm, hid)
     wf_in = load(1, wf_hbm, wf)
-    cot_in = load(2, cot_hbm, cot)
-    wm_in = load(3, wm_hbm, wm)
-    wc_in = load(4, wc_hbm, wc)
+    sends = []
+
+    def send(kind, d, src, slots, base):
+        copy = remote(kind, d, src, slots.at[slot[d] - base], slot[d])
+        copy.start()
+        sends.append(copy)
+
+    def recv(kind, where, src, dst):
+        remote(kind, 0, src, dst, where).wait_recv()
+
+    pl.semaphore_wait(barrier, 8)
+    send(0, 0, hid_hbm.at[pl.ds(0, 3)], r_slot, 0)
+    send(0, 1, hid_hbm.at[pl.ds(13, 3)], r_slot, 0)
     hid_in.wait()
 
-    @pl.loop(0, 16)
+    @pl.loop(0, 16, unroll=4)
     def _(r):
         row_put(s_ext, r + 3, 8, hid[r].astype(F32))
 
@@ -176,31 +186,20 @@
             put(tile, c * 4, col_get(s_ext, 8 + first + c, 3 + row, 8)[:4])
         k_buf[k] = get(tile, 0, 16).astype(BF16)
 
-    pl.semaphore_wait(barrier, 8)
-
-    sends = []
-
-    def send(kind, d, src, slots, base):
-        copy = remote(kind, d, src, slots.at[slot[d] - base], slot[d])
-        copy.start()
-        sends.append(copy)
-
-    def recv(kind, where, src, dst):
-        remote(kind, where, src, dst, where).wait_recv()
-
-    send(0, 0, hid.at[pl.ds(0, 3)], r_slot, 0)
-    send(0, 1, hid.at[pl.ds(13, 3)], r_slot, 0)
     for d in (4, 5, 6, 7):
         send(0, d, k_buf.at[d - 4], k_slot, 4)
     for d in (2, 3):
         send(0, d, c_buf.at[d - 2], c_slot, 2)
 
-    @pl.loop(0, 16)
+    @pl.loop(0, 16, unroll=4)
     def _(r):
         for ph in range(6):
             e_ext[r + 3, ph] = row_get(s_ext, r + 3, 7 + ph, 16, 4).astype(BF16)
 
     wf_in.wait()
+    cot_in = load(2, cot_hbm, cot)
+    wm_in = load(3, wm_hbm, wm)
+    wc_in = load(4, wc_hbm, wc)
     pre[pl.ds(3, 14)] = conv_dot(
         lambda a, b: e_ext[3 + a : 17 + a, b : b + 4].reshape(14 * 64, C), wf
     ).reshape(14, 64, C)
@@ -210,19 +209,19 @@
         row_put(act, i, 0, rounded(a))
         row_put(slp, i, 0, s)
 
-    @pl.loop(3, 17)
+    @pl.loop(3, 17, unroll=2)
     def _(i):
         fine_gelu(i)
 
     cot_in.wait()
 
-    @pl.loop(0, 16)
+    @pl.loop(0, 16, unroll=4)
     def _(r):
         row_put(sx, r, 0, cot[r].astype(F32))
         for p in range(4):
             ctp[r + 1, pl.ds(p * 16, 16)] = row_get(sx, r, p, 16, 4).astype(BF16)
 
-    @pl.loop(0, 8)
+    @pl.loop(0, 8, unroll=4)
     def _(m):
         for p in range(2):
             total = 0.0
@@ -238,92 +237,46 @@
                 total = total + row_get(gma, 2 * q + dr + 2, p * 16, 16)
         row_put(gcax, q + 2, 8, total)
 
-    for side, (row, mid, coarse) in enumerate(((0, 0, 0), (15, 6, 2))):
-        lr_buf[side, pl.ds(0, 64)] = ctp[row + 1]
+    for side, (mid, coarse) in enumerate(((0, 0), (6, 2))):
         for k in range(2):
-            lr_buf[side, pl.ds(64 + 32 * k, 32)] = row_get(gma, mid + k + 2, 0, 32).astype(BF16)
-            lr_buf[side, pl.ds(128 + 16 * k, 16)] = row_get(gcax, coarse + k + 2, 8, 16).astype(BF16)
+            lr_buf[side, pl.ds(32 * k, 32)] = row_get(gma, mid + k + 2, 0, 32).astype(BF16)
+            lr_buf[side, pl.ds(64 + 16 * k, 16)] = row_get(gcax, coarse + k + 2, 8, 16).astype(BF16)
     for side, (col, mids, coarse) in enumerate(((0, (0, 16), 0), (63, (15, 31), 14))):
         put(tile, 0, col_get(sx, col, 0, 16))
         for c in range(2):
             put(tile, 16 + 8 * c, col_get(gma, mids[c], 2, 8))
             put(tile, 32 + 4 * c, col_get(gcax, 8 + coarse + c, 2, 8)[:4])
         lc_buf[side] = get(tile, 0, 48).astype(BF16)
-    for d in (0, 1):
-        send(1, d, lr_buf.at[d], lr_slot, 0)
-    for d in range(2, 8):
-        send(1, d, lc_buf.at[d % 2], lc_slot, 2)
-
-    for k in range(2):
-        recv(0, k, hid.at[pl.ds(0, 3)], r_slot.at[k])
-    for k in range(4):
-        recv(0, 4 + k, k_buf.at[k], k_slot.at[k])
-    for k in range(2):
-        recv(0, 2 + k, c_buf.at[k], c_slot.at[k])
-
-    for j in range(3):
-        row_put(s_ext, 2 - j, 8, r_slot[0, jnp.where(north, j, 2 - j)].astype(F32))
-        row_put(s_ext, 19 + j, 8, r_slot[1, jnp.where(south, 2 - j, j)].astype(F32))
-    for side, first in ((0, -3), (1, 64)):
-        for c in range(3):
-            col_put(s_ext, 8 + first + c, 3, c_slot[side, pl.ds(c * 16, 16)].astype(F32))
-    for k in range(4):
-        put(tile, 0, k_slot[k].astype(F32))
-        first = 64 if k % 2 else -3
-        for c in range(3):
-            for j in range(3):
-                if k < 2:
-                    at, row = jnp.where(north, j, 3 - j), 2 - j
-                else:
-                    at, row = jnp.where(south, 3 - j, j), 19 + j
-                row_put(s_ext, row, 8 + first + c, get(tile, c * 4 + at, 1))
-
-    @pl.loop(0, 6)
-    def _(i):
-        r = i + jnp.where(i >= 3, 16, 0)
-        for ph in range(6):
+        for k, (row, mid, low) in enumerate(((0, 2, 2), (15, 8, 4))):
+            for c in range(2):
+                put(tile, 2 * c, col_get(gma, mids[c], mid, 8)[:2])
+                put(tile, 4 + 2 * c, col_get(gcax, 8 + coarse + c, low, 8)[:2])
+            put(tile, 8, get(sx.ref, row * 64 + col, 1))
+            lk_buf[2 * k + side] = get(tile, 0, 16).astype(BF16)
+
+    side_e, side_l = jnp.where(north, 1, 0), jnp.where(north, 0, 1)
+    sgn_l = jnp.where(north | south, -1, 1)
+
+    def receive(side):
+        recv(0, side, hid.at[pl.ds(0, 3)], r_slot.at[side])
+        for k in range(2):
+            recv(0, 4 + 2 * side + k, k_buf.at[k], k_slot.at[2 * side + k])
+
+    def place(side, first, step, row_order, corner_order):
+        for j in range(3):
+            row_put(s_ext, first + step * j, 8, r_slot[side, row_order(j)].astype(F32))
+        for k in range(2):
+            put(tile, 0, k_slot[2 * side + k].astype(F32))
+            for c in range(3):
+                for j in range(3):
+                    at = (first + step * j) * 80 + 8 + (64 if k else -3) + c
+                    put(s_ext.ref, at, get(tile, c * 4 + corner_order(j), 1))
+
+    def phases(r, which):
+        for ph in which:
             e_ext[r, ph] = row_get(s_ext, r, 7 + ph, 16, 4).astype(BF16)
 
-    for r in (3, 4, 17, 18):
-        for ph in (0, 5):
-            e_ext[r, ph] = row_get(s_ext, r, 7 + ph, 16, 4).astype(BF16)
-
-    edge_rows = lax.broadcasted_iota(jnp.int32, (32, 1), 0)
-    flip = (north & (edge_rows < 2)) | (south & ((edge_rows == 18) | (edge_rows == 19)))
-
-    @pl.loop(0, 10)
-    def _(i):
-        side = i // 5
-        col = 8 - 3 + i + side * 60
-        low, mid, high = (get(s_ext.ref, a * 80 + col, 32, 80) for a in range(3))
-        l_edge[0, i] = jnp.where(flip, high, low).astype(BF16)
-        l_edge[1, i] = mid.astype(BF16)
-        l_edge[2, i] = jnp.where(flip, low, high).astype(BF16)
-
-    def ring(a, b):
-        rows = [1 + sgn_n * (a - 1), 2 + sgn_n * (a - 1), 2 + a, 17 + a, 19 + sgn_s * (a - 1), 20 + sgn_s * (a - 1)]
-        parts = [e_ext[r, b : b + 4].reshape(64, C) for r in rows]
-        parts += [l_edge[a, s * 5 + b : s * 5 + b + 3].reshape(96, C) for s in range(2)]
-        return jnp.concatenate(parts, axis=0)
-
-    res = conv_dot(ring, wf)
-    for k, i in enumerate((0, 1, 2, 17, 18, 19)):
-        pre[i] = res[k * 64 : (k + 1) * 64]
-    pre_e[...] = res[384:].reshape(6, 32, C)
-
-    @pl.loop(0, 6)
-    def _(i):
-        fine_gelu(i + jnp.where(i >= 3, 14, 0))
-        a, s = gelu_pair(pre_e[i])
-        row_put(act_e, i, 0, rounded(a))
-        row_put(slp_e, i, 0, s)
-
-    for dst, src in ((act, act_e), (slp, slp_e)):
-        col_put(dst, 0, 0, row_get(src, 2, 0, 24))
-        col_put(dst, 63, 0, row_get(src, 3, 0, 24))
-
-    @pl.loop(0, 10)
-    def _(m):
+    def pool_row(m):
         for p, shifted in ((0, sm0), (1, sm1)):
             total = 0.0
             for dr in range(2):
@@ -333,29 +286,147 @@
             pf[m, 1 + p] = total.astype(BF16)
             row_put(shifted, m, 8, total)
 
-    for first, shifted, at in ((0, sm1, 7), (4, sm0, 24)):
-        total = 0.0
-        for c in range(2):
-            for dr in range(2):
-                total = total + row_get(act_e, first + c, dr, 16, 2)
-        col_put(shifted, at, 0, 0.25 * total)
-
-    @pl.loop(0, 10)
-    def _(m):
+    def pool_edges():
+        for first, shifted, at in ((0, sm1, 7), (4, sm0, 24)):
+            total = 0.0
+            for c in range(2):
+                for dr in range(2):
+                    total = total + row_get(act_e, first + c, dr, 16, 2)
+            col_put(shifted, at, 0, 0.25 * total)
+
+    def pool_shift(m):
         pf[m, 0] = row_get(sm1, m, 7, 16).astype(BF16)
         pf[m, 3] = row_get(sm0, m, 9, 16).astype(BF16)
 
-    wm_in.wait()
-    pre_m[...] = conv_dot(
-        lambda a, b: pf[a : a + 8, b : b + 2].reshape(256, C), wm
-    ).reshape(8, 32, C)
-
-    @pl.loop(0, 8)
-    def _(m):
+    def mid_gelu(m):
         a, s = gelu_pair(pre_m[m])
         am[m] = rounded(a)
         row_put(slm, m + 2, 0, s)
         slb[m] = s.astype(BF16)
+
+    receive(side_e)
+    for k in range(2):
+        recv(0, 2 + k, c_buf.at[k], c_slot.at[k])
+    for side, first in ((0, -3), (1, 64)):
+        for c in range(3):
+            col_put(s_ext, 8 + first + c, 3, c_slot[side, pl.ds(c * 16, 16)].astype(F32))
+    place(
+        side_e, jnp.where(north, 19, 2), jnp.where(north, 1, -1),
+        lambda j: jnp.where(north, j, 2 - j), lambda j: jnp.where(north, j, 3 - j),
+    )
+    for i in range(3):
+        phases(jnp.where(north, 19, 0) + i, range(6))
+    for r in (3, 4, 17, 18):
+        phases(r, (0, 5))
+
+    @pl.loop(0, 10, unroll=5)
+    def _(i):
+        col = 8 - 3 + i + (i // 5) * 60
+        for a in range(3):
+            l_edge[a, i] = get(s_ext.ref, a * 80 + col, 32, 80).astype(BF16)
+
+    def ring(a, b):
+        parts = [e_ext[jnp.where(north, 20 - q, 1 + q) + a - 1, b : b + 4].reshape(64, C) for q in range(3)]
+        parts += [l_edge[a, s * 5 + b : s * 5 + b + 3].reshape(96, C) for s in range(2)]
+        return jnp.concatenate(parts, axis=0)
+
+    res = conv_dot(ring, wf)
+    for q in range(3):
+        pre[jnp.where(north, 19 - q, q)] = res[q * 64 : (q + 1) * 64]
+    pre_e[...] = res[192:].reshape(6, 32, C)
+
+    @pl.loop(0, 6, unroll=2)
+    def _(i):
+        a, s = gelu_pair(pre_e[i])
+        row_put(act_e, i, 0, rounded(a))
+        row_put(slp_e, i, 0, s)
+
+    for dst, src in ((act, act_e), (slp, slp_e)):
+        col_put(dst, 0, 0, row_get(src, 2, 0, 24))
+        col_put(dst, 63, 0, row_get(src, 3, 0, 24))
+
+    @pl.loop(0, 3, unroll=3)
+    def _(q):
+        fine_gelu(jnp.where(north, 17, 0) + q)
+
+    wm_in.wait()
+
+    @pl.loop(0, 8, unroll=4)
+    def _(i):
+        pool_row(jnp.where(north, 2, 0) + i)
+
+    pool_edges()
+
+    @pl.loop(0, 8, unroll=8)
+    def _(i):
+        pool_shift(jnp.where(north, 2, 0) + i)
+
+    early = jnp.where(north, 2, 0)
+    pre_m[pl.ds(early, 6)] = conv_dot(
+        lambda a, b: pf[pl.ds(early + a, 6), b : b + 2].reshape(192, C), wm
+    ).reshape(6, 32, C)
+
+    @pl.loop(0, 6, unroll=2)
+    def _(i):
+        mid_gelu(early + i)
+
+    receive(side_l)
+    for d in (0, 1):
+        send(1, d, lr_buf.at[d], lr_slot, 0)
+    for d in (2, 3):
+        send(1, d, lc_buf.at[d - 2], lc_slot, 2)
+    for d in (4, 5, 6, 7):
+        send(1, d, lk_buf.at[d - 4], lk_slot, 4)
+
+    place(
+        side_l, jnp.where(north, 2, 19), jnp.where(north, -1, 1),
+        lambda j: jnp.where(south, 2 - j, j), lambda j: jnp.where(south, 3 - j, j),
+    )
+    for i in range(3):
+        phases(jnp.where(north, 0, 19) + i, range(6))
+    edge_first = jnp.where(north, 0, 17)
+    edge_rows = lax.broadcasted_iota(jnp.int32, (16, 1), 0)
+    flip = (north & (edge_rows < 2)) | (south & ((edge_rows == 1) | (edge_rows == 2)))
+
+    @pl.loop(0, 10, unroll=5)
+    def _(i):
+        col = 8 - 3 + i + (i // 5) * 60
+        low, mid, high = (get(s_ext.ref, (edge_first + a) * 80 + col, 16, 80) for a in range(3))
+        l_late[0, i] = jnp.where(flip, high, low).astype(BF16)
+        l_late[1, i] = mid.astype(BF16)
+        l_late[2, i] = jnp.where(flip, low, high).astype(BF16)
+
+    def ring_late(a, b):
+        rows = [jnp.where(north, 1 + q, 20 - q) + (1 if q == 2 else sgn_l) * (a - 1) for q in range(3)]
+        parts = [e_ext[r, b : b + 4].reshape(64, C) for r in rows]
+        parts += [l_late[a, s * 5 + b : s * 5 + b + 3].reshape(48, C) for s in range(2)]
+        return jnp.concatenate(parts, axis=0)
+
+    res = conv_dot(ring_late, wf)
+    for q in range(3):
+        pre[jnp.where(north, q, 19 - q)] = res[q * 64 : (q + 1) * 64]
+    for i in range(6):
+        a, s = gelu_pair(res[192 + 16 * i : 208 + 16 * i])
+        a = rounded(a)
+        for k in range(3):
+            put(act_e.ref, i * act_e.pitch + edge_first + k, a[k : k + 1])
+            put(slp_e.ref, i * slp_e.pitch + edge_first + k, s[k : k + 1])
+
+    @pl.loop(0, 3, unroll=3)
+    def _(q):
+        fine_gelu(jnp.where(north, 0, 17) + q)
+
+    for i in range(2):
+        pool_row(jnp.where(north, 0, 8) + i)
+    pool_edges()
+    for i in range(2):
+        pool_shift(jnp.where(north, 0, 8) + i)
+    late = jnp.where(north, 0, 6)
+    pre_m[pl.ds(late, 2)] = conv_dot(
+        lambda a, b: pf[pl.ds(late + a, 2), b : b + 2].reshape(64, C), wm
+    ).reshape(2, 32, C)
+    for i in range(2):
+        mid_gelu(late + i)
 
     for q in range(4):
         total = 0.0
@@ -371,63 +442,81 @@
         for c in range(2):
             put(tile, 16 + 8 * c, col_get(slm, mids[c], 2, 8))
         pc_buf[side] = get(tile, 0, 32).astype(BF16)
+        for k, row in enumerate((2, 8)):
+            for c in range(2):
+                put(tile, 12 + 2 * c, col_get(slm, mids[c], row, 8)[:2])
+            pk_buf[2 * k + side] = get(tile, 0, 16).astype(BF16)
 
     for d in (0, 1):
         send(2, d, pml.at[pl.ds(d, 3)], pr_slot, 0)
-    for d in (4, 5, 6, 7, 2, 3):
-        send(2, d, pc_buf.at[d % 2], pc_slot, 2)
+    for d in (4, 5, 6, 7):
+        send(2, d, pk_buf.at[d - 4], pk_slot, 4)
+    for d in (2, 3):
+        send(2, d, pc_buf.at[d - 2], pc_slot, 2)
     for d in (0, 1):
         send(3, d, slb.at[pl.ds(6 * d, 2)], sr_slot, 0)
+    for d in (0, 1):
+        send(4, d, ctp.at[1 + 15 * d], ct_slot, 0)
+
+    @pl.loop(0, 16, unroll=4)
+    def _(r):
+        for p in range(4):
+            v = row_get(act, r + 2, p * 16, 16) + am[r // 2, pl.ds((p // 2) * 16, 16)]
+            row_put(ns, r, p, v, 4)
 
     for k in range(2):
         recv(1, k, lr_buf.at[k], lr_slot.at[k])
-    for k in range(6):
+    for k in range(2):
         recv(1, 2 + k, lc_buf.at[0], lc_slot.at[k])
-    for k in range(6):
         put(ts, k * 48, lc_slot[k].astype(F32))
-    ctp[0] = lr_slot[0, pl.ds(0, 64)]
-    ctp[17] = lr_slot[1, pl.ds(0, 64)]
+    for k in range(4):
+        recv(1, 4 + k, lk_buf.at[0], lk_slot.at[k])
+        put(tk, k * 16, lk_slot[k].astype(F32))
 
     def pick(k, at):
         return get(ts, k * 48 + at, 1)
 
-    def edge_columns(dst, base):
+    def corner(k, at):
+        return get(tk, k * 16 + at, 1)
+
+    def edge_columns(dst, base, corner_base):
         for side in range(2):
             for c in range(2):
                 to = side * 2 + c
                 row_put(dst, to, 2, get(ts, side * 48 + base + 8 * c, 8))
                 for j in range(2):
-                    at = base + 8 * c + jnp.where(north, j, 7 - j)
-                    row_put(dst, to, 1 - j, pick(2 + side, at))
-                    at = base + 8 * c + jnp.where(south, 7 - j, j)
-                    row_put(dst, to, 10 + j, pick(4 + side, at))
+                    at = corner_base + 2 * c
+                    row_put(dst, to, 1 - j, corner(side, at + jnp.where(north, j, 1 - j)))
+                    row_put(dst, to, 10 + j, corner(2 + side, at + jnp.where(south, 1 - j, j)))
 
     for j in range(2):
         at_n, at_s = jnp.where(north, j, 1 - j), jnp.where(south, 1 - j, j)
-        row_put(gma, 1 - j, 0, lr_slot[0, pl.ds(pl.multiple_of(64 + 32 * at_n, 32), 32)].astype(F32))
-        row_put(gma, 10 + j, 0, lr_slot[1, pl.ds(pl.multiple_of(64 + 32 * at_s, 32), 32)].astype(F32))
-        row_put(gcax, 1 - j, 8, lr_slot[0, pl.ds(pl.multiple_of(128 + 16 * at_n, 16), 16)].astype(F32))
-        row_put(gcax, 6 + j, 8, lr_slot[1, pl.ds(pl.multiple_of(128 + 16 * at_s, 16), 16)].astype(F32))
+        row_put(gma, 1 - j, 0, lr_slot[0, pl.ds(pl.multiple_of(32 * at_n, 32), 32)].astype(F32))
+        row_put(gma, 10 + j, 0, lr_slot[1, pl.ds(pl.multiple_of(32 * at_s, 32), 32)].astype(F32))
+        row_put(gcax, 1 - j, 8, lr_slot[0, pl.ds(pl.multiple_of(64 + 16 * at_n, 16), 16)].astype(F32))
+        row_put(gcax, 6 + j, 8, lr_slot[1, pl.ds(pl.multiple_of(64 + 16 * at_s, 16), 16)].astype(F32))
     for side in range(2):
         row_put(cte, side, 2, get(ts, side * 48, 16))
-        row_put(cte, side, 1, pick(2 + side, jnp.where(north, 0, 15)))
-        row_put(cte, side, 18, pick(4 + side, jnp.where(south, 15, 0)))
+        row_put(cte, side, 1, corner(side, 8))
+        row_put(cte, side, 18, corner(2 + side, 8))
         for c in range(2):
             col = 8 + (16 if side else -2) + c
             for q in range(4):
                 row_put(gcax, q + 2, col, pick(side, 32 + 4 * c + q))
             for j in range(2):
-                row_put(gcax, 1 - j, col, pick(2 + side, 32 + 4 * c + jnp.where(north, j, 3 - j)))
-                row_put(gcax, 6 + j, col, pick(4 + side, 32 + 4 * c + jnp.where(south, 3 - j, j)))
-    edge_columns(gmae, 16)
+                row_put(gcax, 1 - j, col, corner(side, 4 + 2 * c + jnp.where(north, j, 1 - j)))
+                row_put(gcax, 6 + j, col, corner(2 + side, 4 + 2 * c + jnp.where(south, 1 - j, j)))
+    edge_columns(gmae, 16, 0)
 
     wc_in.wait()
     for k in range(2):
         recv(2, k, pml.at[pl.ds(0, 3)], pr_slot.at[k])
-    for k in range(6):
+    for k in range(2):
         recv(2, 2 + k, pc_buf.at[0], pc_slot.at[k])
-    for k in range(6):
         put(ts, k * 48, pc_slot[k].astype(F32))
+    for k in range(4):
+        recv(2, 4 + k, pk_buf.at[0], pk_slot.at[k])
+        put(tk, k * 16, pk_slot[k].astype(F32))
     for j in range(3):
         row_put(sc, 2 - j, 16, pr_slot[0, jnp.where(north, j, 2 - j)].astype(F32))
         row_put(sc, 7 + j, 16, pr_slot[1, jnp.where(south, 2 - j, j)].astype(F32))
@@ -437,10 +526,10 @@
             for q in range(4):
                 row_put(sc, q + 3, col, pick(side, 4 * c + q))
             for j in range(3):
-                row_put(sc, 2 - j, col, pick(2 + side, 4 * c + jnp.where(north, j, 3 - j)))
-                row_put(sc, 7 + j, col, pick(4 + side, 4 * c + jnp.where(south, 3 - j, j)))
-
-    @pl.loop(0, 10)
+                row_put(sc, 2 - j, col, corner(side, 4 * c + jnp.where(north, j, 3 - j)))
+                row_put(sc, 7 + j, col, corner(2 + side, 4 * c + jnp.where(south, 3 - j, j)))
+
+    @pl.loop(0, 10, unroll=True)
     def _(r):
         for b in range(3):
             cb[b, r] = row_get(sc, r, 7 + b, 32).astype(BF16)
@@ -458,7 +547,7 @@
             ac[i - 2] = rounded(a[8:24])
         row_put(gs, i, 8, row_get(gcax, i, 0, 32) * s)
 
-    @pl.loop(0, 8)
+    @pl.loop(0, 8, unroll=True)
     def _(r):
         for d in range(3):
             gb[d, r] = row_get(gs, r, 7 + d, 32).astype(BF16)
@@ -482,14 +571,20 @@
     for i in range(6):
         row_put(bm, i, 0, 0.25 * res[i * 32 : (i + 1) * 32])
 
+    for q in range(4):
+        for p in range(4):
+            row_put(sx, q, p, ac[q], 4)
+    for r in range(16):
+        out_v[r] = (row_get(ns, r, 0, 64) + row_get(sx, r // 4, 0, 64)).astype(BF16)
+
     for k in range(2):
         recv(3, k, slb.at[pl.ds(0, 2)], sr_slot.at[k])
     for j in range(2):
         row_put(slm, 1 - j, 0, sr_slot[0, jnp.where(north, j, 1 - j)].astype(F32))
         row_put(slm, 10 + j, 0, sr_slot[1, jnp.where(south, 1 - j, j)].astype(F32))
-    edge_columns(sle, 16)
-
-    @pl.loop(0, 12)
+    edge_columns(sle, 16, 12)
+
+    @pl.loop(0, 12, unroll=True)
     def _(k):
         below = row_get(bm, k // 2, 8, 16)
         for p, shifted in ((0, ms0), (1, ms1)):
@@ -512,7 +607,7 @@
     row_put(mc, 2, 0, col_get(ms0, 8, 0, 16))
     row_put(mc, 3, 0, col_get(ms1, 23, 0, 16))
 
-    @pl.loop(0, 12)
+    @pl.loop(0, 12, unroll=True)
     def _(k):
         mg[k, 0] = row_get(ms1, k, 7, 16).astype(BF16)
         mg[k, 3] = row_get(ms0, k, 9, 16).astype(BF16)
@@ -552,7 +647,11 @@
     for side in range(2):
         row_put(bfe, side, 0, res[320 + 16 * side : 336 + 16 * side])
 
-    @pl.loop(0, 18)
+    for k in range(2):
+        recv(4, k, ctp.at[1], ct_slot.at[k])
+        ctp[17 * k] = ct_slot[k]
+
+    @pl.loop(0, 18, unroll=6)
     def _(k):
         for p in range(4):
             g = (
@@ -572,7 +671,7 @@
         row_put(ge, side, 0, g)
         col_put(shifted, at, 0, row_get(ge, side, 1, 24))
 
-    @pl.loop(0, 18)
+    @pl.loop(0, 18, unroll=True)
     def _(k):
         g_ext[k, 0] = row_get(fs3, k, 7, 16).astype(BF16)
         g_ext[k, 5] = row_get(fs0, k, 9, 16).astype(BF16)
@@ -581,38 +680,46 @@
         g_ext[18 + k] = (g_ext[x].astype(F32) + g_ext[y].astype(F32)).astype(BF16)
     g_ext[20] = jnp.zeros((6, 16, C), BF16)
 
-    def fine_t(a, b):
-        ph = slice(2 - b, 6 - b)
-        if a == 1:
-            return g_ext[1:17, ph].reshape(1024, C)
-        if a == 0:
-            top, body, tail = jnp.where(north, 18, 2), 3, jnp.where(south, 20, 17)
-        else:
-            top, body, tail = jnp.where(north, 20, 0), 1, jnp.where(south, 19, 15)
-        parts = [g_ext[top, ph].reshape(64, C), g_ext[body : body + 14, ph].reshape(896, C)]
-        return jnp.concatenate(parts + [g_ext[tail, ph].reshape(64, C)], axis=0)
-
-    pre[pl.ds(0, 16)] = conv_dot_t(fine_t, wf).reshape(16, 64, C)
-
-    @pl.loop(0, 16)
-    def _(r):
-        for p in range(4):
-            v = row_get(act, r + 2, p * 16, 16) + (am[r // 2, pl.ds((p // 2) * 16, 16)] + ac[r // 4])
-            row_put(ns, r, p, v, 4)
-            row_put(sx, r, p, pre[r, pl.ds(p * 16, 16)], 4)
-        out_v[r] = row_get(ns, r, 0, 64).astype(BF16)
-        grad_v[r] = row_get(sx, r, 0, 64).astype(BF16)
-
-    a = load(5, out_v, out_hbm)
-    b = load(6, grad_v, grad_hbm)
     for copy in sends:
         copy.wait_send()
-    a.wait()
-    b.wait()
+
+
+def last_kernel(nlat, out_v, g_ext, wf, out_hbm, grad_hbm, grad_v, sx, sem):
+    lat = lax.axis_index("lat")
+    north = lat == 0
+    south = lat == nlat - 1
+    sx = Rows(sx, 64)
+    copies = [pltpu.make_async_copy(out_v, out_hbm, sem.at[0])]
+    copies[0].start()
+    for h in range(2):
+
+        def fine_t(a, b):
+            ph = slice(2 - b, 6 - b)
+            if a == 1:
+                return g_ext[8 * h + 1 : 8 * h + 9, ph].reshape(512, C)
+            first = 8 * h + 2 - a
+            if h == 0:
+                row = jnp.where(north, 20 if a else 18, first)
+                parts = [g_ext[row, ph].reshape(64, C), g_ext[first + 1 : first + 8, ph].reshape(448, C)]
+            else:
+                row = jnp.where(south, 19 if a else 20, first + 7)
+                parts = [g_ext[first : first + 7, ph].reshape(448, C), g_ext[row, ph].reshape(64, C)]
+            return jnp.concatenate(parts, axis=0)
+
+        res = conv_dot_t(fine_t, wf)
+        for r in range(8):
+            for p in range(4):
+                row_put(sx, 8 * h + r, p, res[r * 64 + p * 16 : r * 64 + p * 16 + 16], 4)
+            grad_v[8 * h + r] = row_get(sx, 8 * h + r, 0, 64).astype(BF16)
+        half = pl.ds(8 * h, 8)
+        copies.append(pltpu.make_async_copy(grad_v.at[half], grad_hbm.at[half], sem.at[1 + h]))
+        copies[-1].start()
+    for copy in copies:
+        copy.wait()
 
 
 def body(nlat, nlon, hidden_in, cotangent, weight_fine, weight_mid, weight_coarse):
-    hbm = pl.BlockSpec(memory_space=pl.ANY)
+    hbm = pl.BlockSpec(memory_space=pltpu.HBM)
     field = (16, 64, C)
     weight = (3, 3, C, C)
 
@@ -623,8 +730,8 @@
         return pltpu.VMEM(shape, F32)
 
     scratch = dict(
-        hid=v(*field), cot=v(*field), wf=v(*weight), wm=v(*weight), wc=v(*weight), out_v=v(*field), grad_v=v(*field),
-        s_ext=f(3, 36 * 80, 128), e_ext=v(22, 6, 16, C), l_edge=v(3, 10, 32, C), pre=f(24, 64, C), pre_e=f(6, 32, C),
+        hid=v(*field), cot=v(*field), wm=v(*weight), wc=v(*weight),
+        s_ext=f(3, 36 * 80, 128), e_ext=v(22, 6, 16, C), l_edge=v(3, 10, 32, C), l_late=v(3, 10, 16, C), pre=f(24, 64, C), pre_e=f(6, 32, C),
         act=f(3, 24 * 64, 128), slp=f(3, 24 * 64, 128), act_e=f(3, 6 * 40, 128), slp_e=f(3, 6 * 32, 128),
         sx=f(3, 16 * 64, 128), ctp=v(18, 64, C), cte=f(3, 2 * 32, 128), gma=f(3, 16 * 32, 128), gmae=f(3, 4 * 16, 128),
         gcax=f(3, 16 * 32, 128),
@@ -632,24 +739,35 @@
         slm=f(3, 16 * 32, 128), sle=f(3, 4 * 16, 128), slb=v(8, 32, C), pml=v(4, 16, C), sc=f(3, 12 * 48, 128),
         cb=v(3, 10, 32, C), ac=f(4, 16, C), gs=f(3, 8 * 48, 128), gb=v(3, 13, 32, C), bm=f(3, 8 * 32, 128),
         mg=v(17, 4, 16, C), ms0=f(3, 16 * 32, 128), ms1=f(3, 16 * 32, 128), mc=f(3, 6 * 24, 128), ml=v(3, 6, 16, C),
-        bfm=f(10, 32, C), bfe=f(3, 2 * 16, 128), g_ext=v(21, 6, 16, C), fs0=f(3, 24 * 32, 128), fs3=f(3, 24 * 32, 128),
-        ge=f(3, 2 * 32, 128), ns=f(3, 16 * 64, 128), tile=f(3, 48, 128), ts=f(3, 288, 128),
+        bfm=f(10, 32, C), bfe=f(3, 2 * 16, 128), fs0=f(3, 24 * 32, 128), fs3=f(3, 24 * 32, 128),
+        ge=f(3, 2 * 32, 128), ns=f(3, 16 * 64, 128), tile=f(3, 48, 128), ts=f(3, 96, 128), tk=f(3, 64, 128),
         c_buf=v(2, 48, C), k_buf=v(4, 16, C), r_slot=v(2, 3, 64, C), c_slot=v(2, 48, C), k_slot=v(4, 16, C),
-        lr_buf=v(2, 160, C), lc_buf=v(2, 48, C), lr_slot=v(2, 160, C), lc_slot=v(6, 48, C),
-        pc_buf=v(2, 32, C), pr_slot=v(2, 3, 16, C), sr_slot=v(2, 2, 32, C), pc_slot=v(6, 32, C),
-        lsem=pltpu.SemaphoreType.DMA((8,)), ssem=pltpu.SemaphoreType.DMA((4, 8)), rsem=pltpu.SemaphoreType.DMA((4, 8)),
+        lr_buf=v(2, 96, C), lc_buf=v(2, 48, C), lk_buf=v(4, 16, C),
+        lr_slot=v(2, 96, C), lc_slot=v(2, 48, C), lk_slot=v(4, 16, C),
+        pc_buf=v(2, 32, C), pk_buf=v(4, 16, C),
+        pr_slot=v(2, 3, 16, C), sr_slot=v(2, 2, 32, C), ct_slot=v(2, 64, C), pc_slot=v(2, 32, C), pk_slot=v(4, 16, C),
+        lsem=pltpu.SemaphoreType.DMA((8,)), ssem=pltpu.SemaphoreType.DMA((5, 8)), rsem=pltpu.SemaphoreType.DMA((5, 8)),
     )
+    vmem = pl.BlockSpec(memory_space=pltpu.VMEM)
+    results = pl.pallas_call(
+        functools.partial(kernel, nlat, nlon),
+        out_shape=(v(*field), v(21, 6, 16, C), v(*weight)),
+        in_specs=[hbm] * 5,
+        out_specs=(vmem, vmem, vmem),
+        scratch_shapes=list(scratch.values()),
+        compiler_params=pltpu.CompilerParams(
+            collective_id=0, has_side_effects=True, vmem_limit_bytes=52 * 2**20
+        ),
+    )(hidden_in, cotangent, weight_fine, weight_mid, weight_coarse)
     shape = jax.ShapeDtypeStruct(field, BF16)
     return pl.pallas_call(
-        functools.partial(kernel, nlat, nlon),
+        functools.partial(last_kernel, nlat),
         out_shape=(shape, shape),
-        in_specs=[hbm] * 5,
+        in_specs=[vmem] * 3,
         out_specs=(hbm, hbm),
-        scratch_shapes=list(scratch.values()),
-        compiler_params=pltpu.CompilerParams(
-            collective_id=0, has_side_effects=True, vmem_limit_bytes=60 * 2**20
-        ),
-    )(hidden_in, cotangent, weight_fine, weight_mid, weight_coarse)
+        scratch_shapes=[v(*field), f(3, 16 * 64, 128), pltpu.SemaphoreType.DMA((3,))],
+        compiler_params=pltpu.CompilerParams(vmem_limit_bytes=40 * 2**20),
+    )(*results)
 
 
 def solution(mesh):

time: 54.4 us -> 47.7 us (0.88)
  the two profiles are of different devices: /device:TPU:1 before, /device:TPU:32 now
where the time goes in v1:
time: 47.7 us; the launch traced here: 47.6 us
  Pallas kernels  46.8 us (98%)
  between operations  0.8 us (2%)
    pallas_call x1, Pallas kernels, body(): pl.pallas_call(functools.partial(kernel, nlat, nlon), out_shape=(v(*field...  42.1 us
    pallas_call x1, Pallas kernels, body(): pl.pallas_call(functools.partial(last_kernel, nlat), out_shape=(shape, sh...  4.72 us

profile of v1, /device:TPU:32, one launch (start us, length us, event | category | flops | bytes accessed | tf_op | source)
XLA Modules:
  0.0 47.6 jit_solution(1882912493961762625)
XLA Ops:
  0.6 42.1 %shard_map.68 = (bf16[16,64,384]{2,1,0:T(8,128)(2,1)S(1)}, bf16[21,6,16,384]{3,2,1,0:T(8,128)(2,1)S(1)}, bf16[3,3,384,384]{3,2,1,0:T(8,128)(2,1)S(1)}) custom-call(bf16[16,64,384]{2,1,0:T(8,128)(2,1)} %hid_hbm.1, bf16[16,64,384]{2,1,0:T(8,128)(2,1)} %cot_hbm.1, bf16[3,3,384,384]{3,2,1,0:T(8,128)(2,1)} %wf_hbm.1, bf16[3,3,384,384]{3,2,1,0:T(8,128)(2,1)} %wm_hbm.1, ...), custom_call_target="tpu_custom_call" | custom-call | tf_op jit(solution)/shard_map/pallas_call | solution.py:752
  42.7 4.7 %shard_map.69 = (bf16[16,64,384]{2,1,0:T(8,128)(2,1)}, bf16[16,64,384]{2,1,0:T(8,128)(2,1)}) custom-call(bf16[16,64,384]{2,1,0:T(8,128)(2,1)S(1)} %get-tuple-element.5.out_v, bf16[21,6,16,384]{3,2,1,0:T(8,128)(2,1)S(1)} %get-tuple-element.6.g_ext, bf16[3,3,384,384]{3,2,1,0:T(8,128)(2,1)S(1)} %get-tuple-element.7.wf), custom_call_target="tpu_custom_call" | custom-call | tf_op jit(solution)/shard_map/pallas_call | solution.py:763

commit v2 on v1

--- a/solution.py
+++ b/solution.py
@@ -84,15 +84,15 @@
 
 def kernel(
     nlat, nlon,
-    hid_hbm, cot_hbm, wf_hbm, wm_hbm, wc_hbm, out_v, g_ext, wf,
+    hid_hbm, cot_hbm, wf_hbm, wm_hbm, wc_hbm, ns, ac, g_ext, wf,
     hid, cot, wm, wc,
     s_ext, e_ext, l_edge, l_late, pre, pre_e, act, slp, act_e, slp_e,
     sx, ctp, cte, gma, gmae, gcax,
-    pf, sm0, sm1, pre_m, am, slm, sle, slb, pml, sc, cb, ac, gs, gb, bm,
-    mg, ms0, ms1, mc, ml, bfm, bfe, fs0, fs3, ge, ns, tile, ts, tk,
-    c_buf, k_buf, r_slot, c_slot, k_slot,
+    pf, sm0, sm1, pre_m, am, slm, sle, slb, pml, sc, cb, gs, gb, bm,
+    mg, ms0, ms1, mc, ml, bfm, bfe, fs0, fs3, ge, tile, ts, tk,
+    c_buf, k_buf, r_slot, c_slot, k_slot, kp_buf, kp_slot,
     lr_buf, lc_buf, lk_buf, lr_slot, lc_slot, lk_slot,
-    pc_buf, pk_buf, pr_slot, sr_slot, ct_slot, pc_slot, pk_slot,
+    pc_buf, pk_buf, p2_buf, p2_slot, sl_buf, sl_slot, pr_slot, sr_slot, ct_slot, pc_slot, pk_slot,
     lsem, ssem, rsem,
 ):
     s_ext = Rows(s_ext, 80)
@@ -142,10 +142,10 @@
         jnp.where(south, 7, 5), jnp.where(south, 6, 4),
     ]
 
-    def remote(kind, d, src, dst, where):
+    def remote(kind, d, src, dst, where, target):
         return pltpu.make_async_remote_copy(
             src_ref=src, dst_ref=dst, send_sem=ssem.at[kind, d], recv_sem=rsem.at[kind, where],
-            device_id=there[d], device_id_type=MESH,
+            device_id=target, device_id_type=MESH,
         )
 
     def load(i, src, dst):
@@ -162,16 +162,34 @@
     sends = []
 
     def send(kind, d, src, slots, base):
-        copy = remote(kind, d, src, slots.at[slot[d] - base], slot[d])
+        copy = remote(kind, d, src, slots.at[slot[d] - base], slot[d], there[d])
         copy.start()
         sends.append(copy)
 
     def recv(kind, where, src, dst):
-        remote(kind, 0, src, dst, where).wait_recv()
+        remote(kind, 0, src, dst, where, there[0]).wait_recv()
 
     pl.semaphore_wait(barrier, 8)
-    send(0, 0, hid_hbm.at[pl.ds(0, 3)], r_slot, 0)
-    send(0, 1, hid_hbm.at[pl.ds(13, 3)], r_slot, 0)
+    pole = north | south
+    far = {k: jnp.where(north, there[0][k], there[1][k]) for k in ("lat", "lon")}
+    near = {k: jnp.where(north, there[1][k], there[0][k]) for k in ("lat", "lon")}
+    far_slot, near_slot = jnp.where(north, slot[0], slot[1]), jnp.where(north, slot[1], slot[0])
+
+    def far_rows(n):
+        src = hid_hbm.at[pl.ds(jnp.where(north, 0, 16 - n), n)]
+        return remote(0, 0, src, r_slot.at[far_slot, pl.ds(0, n)], far_slot, far)
+
+    @pl.when(pole)
+    def _():
+        far_rows(1).start()
+
+    @pl.when(jnp.logical_not(pole))
+    def _():
+        far_rows(3).start()
+
+    copy = remote(0, 1, hid_hbm.at[pl.ds(jnp.where(north, 13, 0), 3)], r_slot.at[near_slot], near_slot, near)
+    copy.start()
+    sends.append(copy)
     hid_in.wait()
 
     @pl.loop(0, 16, unroll=4)
@@ -186,8 +204,35 @@
             put(tile, c * 4, col_get(s_ext, 8 + first + c, 3 + row, 8)[:4])
         k_buf[k] = get(tile, 0, 16).astype(BF16)
 
-    for d in (4, 5, 6, 7):
-        send(0, d, k_buf.at[d - 4], k_slot, 4)
+    for side, first in ((0, 0), (1, 61)):
+        at = (3 + jnp.where(north, 0, 15)) * 80 + 8 + first
+        for c in range(3):
+            for l in range(LANES):
+                tile[0, pl.ds(3 * c + l, 1), :] = s_ext.ref[l, pl.ds(at + c, 1), :]
+        kp_buf[side] = tile[0, pl.ds(0, 16), :].astype(BF16)
+
+    def corner_copy(side, at_far, small):
+        top = north if at_far else jnp.logical_not(north)
+        target = {k: jnp.where(top, there[4 + side][k], there[6 + side][k]) for k in ("lat", "lon")}
+        to = jnp.where(top, slot[4 + side], slot[6 + side])
+        if small:
+            return remote(0, 4 + side, kp_buf.at[side], kp_slot.at[to - 4], to, target)
+        src = k_buf.at[side + jnp.where(top, 0, 2)]
+        return remote(0, (4 if at_far else 6) + side, src, k_slot.at[to - 4], to, target)
+
+    @pl.when(pole)
+    def _():
+        for side in range(2):
+            corner_copy(side, True, True).start()
+
+    @pl.when(jnp.logical_not(pole))
+    def _():
+        for side in range(2):
+            corner_copy(side, True, False).start()
+
+    for side in range(2):
+        sends.append(corner_copy(side, False, False))
+        sends[-1].start()
     for d in (2, 3):
         send(0, d, c_buf.at[d - 2], c_slot, 2)
 
@@ -209,9 +254,120 @@
         row_put(act, i, 0, rounded(a))
         row_put(slp, i, 0, s)
 
+    side_e, side_l = jnp.where(north, 1, 0), jnp.where(north, 0, 1)
+    sgn_l = jnp.where(north | south, -1, 1)
+
+    def receive(side):
+        recv(0, side, hid.at[pl.ds(0, 3)], r_slot.at[side])
+        for k in range(2):
+            recv(0, 4 + 2 * side + k, k_buf.at[k], k_slot.at[2 * side + k])
+
+    def place(side, first, step, row_order, corner_order):
+        for j in range(3):
+            row_put(s_ext, first + step * j, 8, r_slot[side, row_order(j)].astype(F32))
+        for k in range(2):
+            put(tile, 0, k_slot[2 * side + k].astype(F32))
+            for c in range(3):
+                for j in range(3):
+                    at = (first + step * j) * 80 + 8 + (64 if k else -3) + c
+                    put(s_ext.ref, at, get(tile, c * 4 + corner_order(j), 1))
+
+    def phases(r, which):
+        for ph in which:
+            e_ext[r, ph] = row_get(s_ext, r, 7 + ph, 16, 4).astype(BF16)
+
+    def pool_row(m):
+        for p, shifted in ((0, sm0), (1, sm1)):
+            total = 0.0
+            for dr in range(2):
+                for dp in range(2):
+                    total = total + row_get(act, 2 * m + dr, (2 * p + dp) * 16, 16)
+            total = 0.25 * total
+            pf[m, 1 + p] = total.astype(BF16)
+            row_put(shifted, m, 8, total)
+
+    def pool_edges():
+        for first, shifted, at in ((0, sm1, 7), (4, sm0, 24)):
+            total = 0.0
+            for c in range(2):
+                for dr in range(2):
+                    total = total + row_get(act_e, first + c, dr, 16, 2)
+            col_put(shifted, at, 0, 0.25 * total)
+
+    def pool_shift(m):
+        pf[m, 0] = row_get(sm1, m, 7, 16).astype(BF16)
+        pf[m, 3] = row_get(sm0, m, 9, 16).astype(BF16)
+
+    def mid_gelu(m):
+        a, s = gelu_pair(pre_m[m])
+        am[m] = rounded(a)
+        row_put(slm, m + 2, 0, s)
+        slb[m] = s.astype(BF16)
+
+    for k in range(2):
+        recv(0, 2 + k, c_buf.at[k], c_slot.at[k])
+    for side, first in ((0, -3), (1, 64)):
+        for c in range(3):
+            col_put(s_ext, 8 + first + c, 3, c_slot[side, pl.ds(c * 16, 16)].astype(F32))
+    for r in (3, 4, 17, 18):
+        phases(r, (0, 5))
+
     @pl.loop(3, 17, unroll=2)
     def _(i):
         fine_gelu(i)
+
+    pole_row = jnp.where(north, 2, 17)
+    beyond_row = jnp.where(north, 1, 18)
+
+    @pl.when(pole)
+    def _():
+        recv(0, side_l, hid.at[pl.ds(0, 1)], r_slot.at[side_l, pl.ds(0, 1)])
+        halo = jnp.where(north, 2, 19)
+        row_put(s_ext, halo, 8, r_slot[side_l, 0].astype(F32))
+        for k in range(2):
+            recv(0, 4 + 2 * side_l + k, kp_buf.at[k], kp_slot.at[2 * side_l + k])
+            tile[0, pl.ds(0, 16), :] = kp_slot[2 * side_l + k].astype(F32)
+            for c in range(3):
+                at = halo * 80 + 8 + (64 if k else -3) + c
+                for l in range(LANES):
+                    s_ext.ref[l, pl.ds(at, 1), :] = tile[0, pl.ds(3 * c + l, 1), :]
+        phases(halo, range(6))
+        two = jnp.where(north, 2, 16)
+
+        @pl.loop(0, 10, unroll=5)
+        def _(i):
+            col = 8 - 3 + i + (i // 5) * 60
+            for a in range(3):
+                l_late[a, i] = get(s_ext.ref, (two + a) * 80 + col, 16, 80).astype(BF16)
+
+        def ring_pole(a, b):
+            parts = [e_ext[pole_row + a, b : b + 4].reshape(64, C)]
+            parts += [l_late[a, s * 5 + b : s * 5 + b + 3].reshape(48, C) for s in range(2)]
+            return jnp.concatenate(parts, axis=0)
+
+        res = conv_dot(ring_pole, wf)
+        pre[pole_row] = res[:64]
+        fine_gelu(pole_row)
+        for i in range(6):
+            a, s = gelu_pair(res[64 + 16 * i : 80 + 16 * i])
+            a = rounded(a)
+            for k in range(2):
+                put(act_e.ref, i * act_e.pitch + two + k, a[k : k + 1])
+                put(slp_e.ref, i * slp_e.pitch + two + k, s[k : k + 1])
+                if i in (2, 3):
+                    put(act.ref, (two + k) * act.pitch + (63 if i == 3 else 0), a[k : k + 1])
+        m = jnp.where(north, 1, 8)
+        pool_row(m)
+        pool_edges()
+        pool_shift(m)
+        put(tile, 0, row_get(sm0, m, 8, 16))
+        put(tile, 16, row_get(sm1, m, 8, 16))
+        put(tile, 32, row_get(sm1, m, 7, 1))
+        put(tile, 33, row_get(sm0, m, 24, 1))
+        for side in range(2):
+            put(tile, 34 + side, get(slp_e.ref, (1 + 3 * side) * slp_e.pitch + pole_row, 1))
+        p2_buf[...] = get(tile, 0, 48).astype(BF16)
+        remote(5, 0, p2_buf, p2_slot, 0, far).start()
 
     cot_in.wait()
 
@@ -254,70 +410,21 @@
             put(tile, 8, get(sx.ref, row * 64 + col, 1))
             lk_buf[2 * k + side] = get(tile, 0, 16).astype(BF16)
 
-    side_e, side_l = jnp.where(north, 1, 0), jnp.where(north, 0, 1)
-    sgn_l = jnp.where(north | south, -1, 1)
-
-    def receive(side):
-        recv(0, side, hid.at[pl.ds(0, 3)], r_slot.at[side])
-        for k in range(2):
-            recv(0, 4 + 2 * side + k, k_buf.at[k], k_slot.at[2 * side + k])
-
-    def place(side, first, step, row_order, corner_order):
-        for j in range(3):
-            row_put(s_ext, first + step * j, 8, r_slot[side, row_order(j)].astype(F32))
-        for k in range(2):
-            put(tile, 0, k_slot[2 * side + k].astype(F32))
-            for c in range(3):
-                for j in range(3):
-                    at = (first + step * j) * 80 + 8 + (64 if k else -3) + c
-                    put(s_ext.ref, at, get(tile, c * 4 + corner_order(j), 1))
-
-    def phases(r, which):
-        for ph in which:
-            e_ext[r, ph] = row_get(s_ext, r, 7 + ph, 16, 4).astype(BF16)
-
-    def pool_row(m):
-        for p, shifted in ((0, sm0), (1, sm1)):
-            total = 0.0
-            for dr in range(2):
-                for dp in range(2):
-                    total = total + row_get(act, 2 * m + dr, (2 * p + dp) * 16, 16)
-            total = 0.25 * total
-            pf[m, 1 + p] = total.astype(BF16)
-            row_put(shifted, m, 8, total)
-
-    def pool_edges():
-        for first, shifted, at in ((0, sm1, 7), (4, sm0, 24)):
-            total = 0.0
-            for c in range(2):
-                for dr in range(2):
-                    total = total + row_get(act_e, first + c, dr, 16, 2)
-            col_put(shifted, at, 0, 0.25 * total)
-
-    def pool_shift(m):
-        pf[m, 0] = row_get(sm1, m, 7, 16).astype(BF16)
-        pf[m, 3] = row_get(sm0, m, 9, 16).astype(BF16)
-
-    def mid_gelu(m):
-        a, s = gelu_pair(pre_m[m])
-        am[m] = rounded(a)
-        row_put(slm, m + 2, 0, s)
-        slb[m] = s.astype(BF16)
+    for d in (0, 1):
+        send(1, d, lr_buf.at[d], lr_slot, 0)
+    for d in (2, 3):
+        send(1, d, lc_buf.at[d - 2], lc_slot, 2)
+    for d in (4, 5, 6, 7):
+        send(1, d, lk_buf.at[d - 4], lk_slot, 4)
+
 
     receive(side_e)
-    for k in range(2):
-        recv(0, 2 + k, c_buf.at[k], c_slot.at[k])
-    for side, first in ((0, -3), (1, 64)):
-        for c in range(3):
-            col_put(s_ext, 8 + first + c, 3, c_slot[side, pl.ds(c * 16, 16)].astype(F32))
     place(
         side_e, jnp.where(north, 19, 2), jnp.where(north, 1, -1),
         lambda j: jnp.where(north, j, 2 - j), lambda j: jnp.where(north, j, 3 - j),
     )
     for i in range(3):
         phases(jnp.where(north, 19, 0) + i, range(6))
-    for r in (3, 4, 17, 18):
-        phases(r, (0, 5))
 
     @pl.loop(0, 10, unroll=5)
     def _(i):
@@ -370,57 +477,67 @@
     def _(i):
         mid_gelu(early + i)
 
-    receive(side_l)
-    for d in (0, 1):
-        send(1, d, lr_buf.at[d], lr_slot, 0)
-    for d in (2, 3):
-        send(1, d, lc_buf.at[d - 2], lc_slot, 2)
-    for d in (4, 5, 6, 7):
-        send(1, d, lk_buf.at[d - 4], lk_slot, 4)
-
-    place(
-        side_l, jnp.where(north, 2, 19), jnp.where(north, -1, 1),
-        lambda j: jnp.where(south, 2 - j, j), lambda j: jnp.where(south, 3 - j, j),
-    )
-    for i in range(3):
-        phases(jnp.where(north, 0, 19) + i, range(6))
-    edge_first = jnp.where(north, 0, 17)
-    edge_rows = lax.broadcasted_iota(jnp.int32, (16, 1), 0)
-    flip = (north & (edge_rows < 2)) | (south & ((edge_rows == 1) | (edge_rows == 2)))
-
-    @pl.loop(0, 10, unroll=5)
-    def _(i):
-        col = 8 - 3 + i + (i // 5) * 60
-        low, mid, high = (get(s_ext.ref, (edge_first + a) * 80 + col, 16, 80) for a in range(3))
-        l_late[0, i] = jnp.where(flip, high, low).astype(BF16)
-        l_late[1, i] = mid.astype(BF16)
-        l_late[2, i] = jnp.where(flip, low, high).astype(BF16)
-
-    def ring_late(a, b):
-        rows = [jnp.where(north, 1 + q, 20 - q) + (1 if q == 2 else sgn_l) * (a - 1) for q in range(3)]
-        parts = [e_ext[r, b : b + 4].reshape(64, C) for r in rows]
-        parts += [l_late[a, s * 5 + b : s * 5 + b + 3].reshape(48, C) for s in range(2)]
-        return jnp.concatenate(parts, axis=0)
-
-    res = conv_dot(ring_late, wf)
-    for q in range(3):
-        pre[jnp.where(north, q, 19 - q)] = res[q * 64 : (q + 1) * 64]
-    for i in range(6):
-        a, s = gelu_pair(res[192 + 16 * i : 208 + 16 * i])
-        a = rounded(a)
-        for k in range(3):
-            put(act_e.ref, i * act_e.pitch + edge_first + k, a[k : k + 1])
-            put(slp_e.ref, i * slp_e.pitch + edge_first + k, s[k : k + 1])
-
-    @pl.loop(0, 3, unroll=3)
-    def _(q):
-        fine_gelu(jnp.where(north, 0, 17) + q)
-
-    for i in range(2):
-        pool_row(jnp.where(north, 0, 8) + i)
-    pool_edges()
-    for i in range(2):
-        pool_shift(jnp.where(north, 0, 8) + i)
+    @pl.when(jnp.logical_not(pole))
+    def _():
+        receive(side_l)
+        place(
+            side_l, jnp.where(north, 2, 19), jnp.where(north, -1, 1),
+            lambda j: jnp.where(south, 2 - j, j), lambda j: jnp.where(south, 3 - j, j),
+        )
+        for i in range(3):
+            phases(jnp.where(north, 0, 19) + i, range(6))
+        edge_first = jnp.where(north, 0, 17)
+        edge_rows = lax.broadcasted_iota(jnp.int32, (16, 1), 0)
+        flip = (north & (edge_rows < 2)) | (south & ((edge_rows == 1) | (edge_rows == 2)))
+
+        @pl.loop(0, 10, unroll=5)
+        def _(i):
+            col = 8 - 3 + i + (i // 5) * 60
+            low, mid, high = (get(s_ext.ref, (edge_first + a) * 80 + col, 16, 80) for a in range(3))
+            l_late[0, i] = jnp.where(flip, high, low).astype(BF16)
+            l_late[1, i] = mid.astype(BF16)
+            l_late[2, i] = jnp.where(flip, low, high).astype(BF16)
+
+        def ring_late(a, b):
+            rows = [jnp.where(north, 1 + q, 20 - q) + (1 if q == 2 else sgn_l) * (a - 1) for q in range(3)]
+            parts = [e_ext[r, b : b + 4].reshape(64, C) for r in rows]
+            parts += [l_late[a, s * 5 + b : s * 5 + b + 3].reshape(48, C) for s in range(2)]
+            return jnp.concatenate(parts, axis=0)
+
+        res = conv_dot(ring_late, wf)
+        for q in range(3):
+            pre[jnp.where(north, q, 19 - q)] = res[q * 64 : (q + 1) * 64]
+        for i in range(6):
+            a, s = gelu_pair(res[192 + 16 * i : 208 + 16 * i])
+            a = rounded(a)
+            for k in range(3):
+                put(act_e.ref, i * act_e.pitch + edge_first + k, a[k : k + 1])
+                put(slp_e.ref, i * slp_e.pitch + edge_first + k, s[k : k + 1])
+
+        @pl.loop(0, 3, unroll=3)
+        def _(q):
+            fine_gelu(jnp.where(north, 0, 17) + q)
+
+        for i in range(2):
+            pool_row(jnp.where(north, 0, 8) + i)
+        pool_edges()
+        for i in range(2):
+            pool_shift(jnp.where(north, 0, 8) + i)
+
+    @pl.when(pole)
+    def _():
+        recv(5, 0, p2_buf, p2_slot)
+        m = jnp.where(north, 0, 9)
+        put(tile, 0, p2_slot[...].astype(F32))
+        for p, shifted in ((0, sm0), (1, sm1)):
+            pf[m, 1 + p] = p2_slot[pl.ds(16 * p, 16)]
+            row_put(shifted, m, 8, get(tile, 16 * p, 16))
+        put(sm1.ref, m * sm1.pitch + 7, get(tile, 32, 1))
+        put(sm0.ref, m * sm0.pitch + 24, get(tile, 33, 1))
+        pool_shift(m)
+        for side in range(2):
+            put(slp_e.ref, (1 + 3 * side) * slp_e.pitch + beyond_row, get(tile, 34 + side, 1))
+
     late = jnp.where(north, 0, 6)
     pre_m[pl.ds(late, 2)] = conv_dot(
         lambda a, b: pf[pl.ds(late + a, 2), b : b + 2].reshape(64, C), wm
@@ -447,8 +564,11 @@
                 put(tile, 12 + 2 * c, col_get(slm, mids[c], row, 8)[:2])
             pk_buf[2 * k + side] = get(tile, 0, 16).astype(BF16)
 
-    for d in (0, 1):
-        send(2, d, pml.at[pl.ds(d, 3)], pr_slot, 0)
+    far_d, near_d = jnp.where(north, 0, 1), jnp.where(north, 1, 0)
+    for d, first, to, target in ((0, far_d, far_slot, far), (1, near_d, near_slot, near)):
+        copy = remote(2, d, pml.at[pl.ds(first, 3)], pr_slot.at[to], to, target)
+        copy.start()
+        sends.append(copy)
     for d in (4, 5, 6, 7):
         send(2, d, pk_buf.at[d - 4], pk_slot, 4)
     for d in (2, 3):
@@ -457,6 +577,11 @@
         send(3, d, slb.at[pl.ds(6 * d, 2)], sr_slot, 0)
     for d in (0, 1):
         send(4, d, ctp.at[1 + 15 * d], ct_slot, 0)
+    @pl.when(pole)
+    def _():
+        sl_buf[...] = row_get(slp, pole_row, 0, 64).astype(BF16)
+        remote(6, 0, sl_buf, sl_slot, 0, far).start()
+
 
     @pl.loop(0, 16, unroll=4)
     def _(r):
@@ -571,12 +696,6 @@
     for i in range(6):
         row_put(bm, i, 0, 0.25 * res[i * 32 : (i + 1) * 32])
 
-    for q in range(4):
-        for p in range(4):
-            row_put(sx, q, p, ac[q], 4)
-    for r in range(16):
-        out_v[r] = (row_get(ns, r, 0, 64) + row_get(sx, r // 4, 0, 64)).astype(BF16)
-
     for k in range(2):
         recv(3, k, slb.at[pl.ds(0, 2)], sr_slot.at[k])
     for j in range(2):
@@ -651,6 +770,11 @@
         recv(4, k, ctp.at[1], ct_slot.at[k])
         ctp[17 * k] = ct_slot[k]
 
+    @pl.when(pole)
+    def _():
+        recv(6, 0, sl_buf, sl_slot)
+        row_put(slp, beyond_row, 0, sl_slot[...].astype(F32))
+
     @pl.loop(0, 18, unroll=6)
     def _(k):
         for p in range(4):
@@ -683,14 +807,27 @@
     for copy in sends:
         copy.wait_send()
 
-
-def last_kernel(nlat, out_v, g_ext, wf, out_hbm, grad_hbm, grad_v, sx, sem):
+    @pl.when(pole)
+    def _():
+        far_rows(1).wait_send()
+        for side in range(2):
+            corner_copy(side, True, True).wait_send()
+        remote(5, 0, p2_buf, p2_slot, 0, far).wait_send()
+        remote(6, 0, sl_buf, sl_slot, 0, far).wait_send()
+
+    @pl.when(jnp.logical_not(pole))
+    def _():
+        far_rows(3).wait_send()
+        for side in range(2):
+            corner_copy(side, True, False).wait_send()
+
+
+def last_kernel(nlat, ns, ac, g_ext, wf, out_hbm, grad_hbm, out_v, grad_v, sx, acx, sem):
     lat = lax.axis_index("lat")
     north = lat == 0
     south = lat == nlat - 1
-    sx = Rows(sx, 64)
-    copies = [pltpu.make_async_copy(out_v, out_hbm, sem.at[0])]
-    copies[0].start()
+    sx, ns, acx = Rows(sx, 64), Rows(ns, 64), Rows(acx, 64)
+    copies = []
     for h in range(2):
 
         def fine_t(a, b):
@@ -707,12 +844,20 @@
             return jnp.concatenate(parts, axis=0)
 
         res = conv_dot_t(fine_t, wf)
+        if h == 0:
+            for q in range(4):
+                for p in range(4):
+                    row_put(acx, q, p, ac[q], 4)
+            for r in range(16):
+                out_v[r] = (row_get(ns, r, 0, 64) + row_get(acx, r // 4, 0, 64)).astype(BF16)
+            copies.append(pltpu.make_async_copy(out_v, out_hbm, sem.at[2]))
+            copies[-1].start()
         for r in range(8):
             for p in range(4):
                 row_put(sx, 8 * h + r, p, res[r * 64 + p * 16 : r * 64 + p * 16 + 16], 4)
             grad_v[8 * h + r] = row_get(sx, 8 * h + r, 0, 64).astype(BF16)
         half = pl.ds(8 * h, 8)
-        copies.append(pltpu.make_async_copy(grad_v.at[half], grad_hbm.at[half], sem.at[1 + h]))
+        copies.append(pltpu.make_async_copy(grad_v.at[half], grad_hbm.at[half], sem.at[h]))
         copies[-1].start()
     for copy in copies:
         copy.wait()
@@ -737,23 +882,25 @@
         gcax=f(3, 16 * 32, 128),
         pf=v(10, 4, 16, C), sm0=f(3, 16 * 32, 128), sm1=f(3, 16 * 32, 128), pre_m=f(8, 32, C), am=f(8, 32, C),
         slm=f(3, 16 * 32, 128), sle=f(3, 4 * 16, 128), slb=v(8, 32, C), pml=v(4, 16, C), sc=f(3, 12 * 48, 128),
-        cb=v(3, 10, 32, C), ac=f(4, 16, C), gs=f(3, 8 * 48, 128), gb=v(3, 13, 32, C), bm=f(3, 8 * 32, 128),
+        cb=v(3, 10, 32, C), gs=f(3, 8 * 48, 128), gb=v(3, 13, 32, C), bm=f(3, 8 * 32, 128),
         mg=v(17, 4, 16, C), ms0=f(3, 16 * 32, 128), ms1=f(3, 16 * 32, 128), mc=f(3, 6 * 24, 128), ml=v(3, 6, 16, C),
         bfm=f(10, 32, C), bfe=f(3, 2 * 16, 128), fs0=f(3, 24 * 32, 128), fs3=f(3, 24 * 32, 128),
-        ge=f(3, 2 * 32, 128), ns=f(3, 16 * 64, 128), tile=f(3, 48, 128), ts=f(3, 96, 128), tk=f(3, 64, 128),
+        ge=f(3, 2 * 32, 128), tile=f(3, 48, 128), ts=f(3, 96, 128), tk=f(3, 64, 128),
         c_buf=v(2, 48, C), k_buf=v(4, 16, C), r_slot=v(2, 3, 64, C), c_slot=v(2, 48, C), k_slot=v(4, 16, C),
+        kp_buf=v(2, 16, 128), kp_slot=v(4, 16, 128),
         lr_buf=v(2, 96, C), lc_buf=v(2, 48, C), lk_buf=v(4, 16, C),
         lr_slot=v(2, 96, C), lc_slot=v(2, 48, C), lk_slot=v(4, 16, C),
         pc_buf=v(2, 32, C), pk_buf=v(4, 16, C),
+        p2_buf=v(48, C), p2_slot=v(48, C), sl_buf=v(64, C), sl_slot=v(64, C),
         pr_slot=v(2, 3, 16, C), sr_slot=v(2, 2, 32, C), ct_slot=v(2, 64, C), pc_slot=v(2, 32, C), pk_slot=v(4, 16, C),
-        lsem=pltpu.SemaphoreType.DMA((8,)), ssem=pltpu.SemaphoreType.DMA((5, 8)), rsem=pltpu.SemaphoreType.DMA((5, 8)),
+        lsem=pltpu.SemaphoreType.DMA((8,)), ssem=pltpu.SemaphoreType.DMA((7, 8)), rsem=pltpu.SemaphoreType.DMA((7, 8)),
     )
     vmem = pl.BlockSpec(memory_space=pltpu.VMEM)
     results = pl.pallas_call(
         functools.partial(kernel, nlat, nlon),
-        out_shape=(v(*field), v(21, 6, 16, C), v(*weight)),
+        out_shape=(f(3, 16 * 64, 128), f(4, 16, C), v(21, 6, 16, C), v(*weight)),
         in_specs=[hbm] * 5,
-        out_specs=(vmem, vmem, vmem),
+        out_specs=(vmem,) * 4,
         scratch_shapes=list(scratch.values()),
         compiler_params=pltpu.CompilerParams(
             collective_id=0, has_side_effects=True, vmem_limit_bytes=52 * 2**20
@@ -763,10 +910,10 @@
     return pl.pallas_call(
         functools.partial(last_kernel, nlat),
         out_shape=(shape, shape),
-        in_specs=[vmem] * 3,
+        in_specs=[vmem] * 4,
         out_specs=(hbm, hbm),
-        scratch_shapes=[v(*field), f(3, 16 * 64, 128), pltpu.SemaphoreType.DMA((3,))],
-        compiler_params=pltpu.CompilerParams(vmem_limit_bytes=40 * 2**20),
+        scratch_shapes=[v(*field), v(*field), f(3, 16 * 64, 128), f(3, 4 * 64, 128), pltpu.SemaphoreType.DMA((3,))],
+        compiler_params=pltpu.CompilerParams(vmem_limit_bytes=36 * 2**20),
     )(*results)
 
 

time: 47.7 us -> 45.9 us (0.962)
  the two profiles are of different devices: /device:TPU:32 before, /device:TPU:1 now
where the time goes in v2:
time: 45.9 us; the launch traced here: 45.8 us
  Pallas kernels  45 us (98%)
  between operations  0.8 us (2%)
    pallas_call x1, Pallas kernels, body(): pl.pallas_call(functools.partial(kernel, nlat, nlon), out_shape=(f(3, 16...  39.9 us
    pallas_call x1, Pallas kernels, body(): pl.pallas_call(functools.partial(last_kernel, nlat), out_shape=(shape, sh...  5.05 us

profile of v2, /device:TPU:1, one launch (start us, length us, event | category | flops | bytes accessed | tf_op | source)
XLA Modules:
  0.0 45.8 jit_solution(12972338005615573950)
XLA Ops:
  0.6 39.9 %shard_map.68 = (f32[3,1024,128]{2,1,0:T(8,128)S(1)}, f32[4,16,384]{2,1,0:T(8,128)S(1)}, bf16[21,6,16,384]{3,2,1,0:T(8,128)(2,1)S(1)}, bf16[3,3,384,384]{3,2,1,0:T(8,128)(2,1)S(1)}) custom-call(bf16[16,64,384]{2,1,0:T(8,128)(2,1)} %hid_hbm.1, bf16[16,64,384]{2,1,0:T(8,128)(2,1)} %cot_hbm.1, bf16[3,3,384,384]{3,2,1,0:T(8,128)(2,1)} %wf_hbm.1, ...), custom_call_target="tpu_custom_call" | custom-call | tf_op jit(solution)/shard_map/pallas_call | solution.py:899
  40.6 5.0 %shard_map.69 = (bf16[16,64,384]{2,1,0:T(8,128)(2,1)}, bf16[16,64,384]{2,1,0:T(8,128)(2,1)}) custom-call(f32[3,1024,128]{2,1,0:T(8,128)S(1)} %get-tuple-element.6.ns, f32[4,16,384]{2,1,0:T(8,128)S(1)} %get-tuple-element.7.ac, bf16[21,6,16,384]{3,2,1,0:T(8,128)(2,1)S(1)} %get-tuple-element.8.g_ext, bf16[3,3,384,384]{3,2,1,0:T(8,128)(2,1)S(1)} %get-tuple-element.9.wf), custom_call_target="tpu_custom_call" | custom-call | tf_op jit(solution)/shard_map/pallas_call | solution.py:910

commit v3 on v2

--- a/solution.py
+++ b/solution.py
@@ -877,15 +877,15 @@
     scratch = dict(
         hid=v(*field), cot=v(*field), wm=v(*weight), wc=v(*weight),
         s_ext=f(3, 36 * 80, 128), e_ext=v(22, 6, 16, C), l_edge=v(3, 10, 32, C), l_late=v(3, 10, 16, C), pre=f(24, 64, C), pre_e=f(6, 32, C),
-        act=f(3, 24 * 64, 128), slp=f(3, 24 * 64, 128), act_e=f(3, 6 * 40, 128), slp_e=f(3, 6 * 32, 128),
-        sx=f(3, 16 * 64, 128), ctp=v(18, 64, C), cte=f(3, 2 * 32, 128), gma=f(3, 16 * 32, 128), gmae=f(3, 4 * 16, 128),
+        act=f(3, 25 * 64, 128), slp=f(3, 25 * 64, 128), act_e=f(3, 6 * 40, 128), slp_e=f(3, 6 * 32, 128),
+        sx=f(3, 17 * 64, 128), ctp=v(18, 64, C), cte=f(3, 2 * 32, 128), gma=f(3, 17 * 32, 128), gmae=f(3, 5 * 16, 128),
         gcax=f(3, 16 * 32, 128),
-        pf=v(10, 4, 16, C), sm0=f(3, 16 * 32, 128), sm1=f(3, 16 * 32, 128), pre_m=f(8, 32, C), am=f(8, 32, C),
-        slm=f(3, 16 * 32, 128), sle=f(3, 4 * 16, 128), slb=v(8, 32, C), pml=v(4, 16, C), sc=f(3, 12 * 48, 128),
-        cb=v(3, 10, 32, C), gs=f(3, 8 * 48, 128), gb=v(3, 13, 32, C), bm=f(3, 8 * 32, 128),
-        mg=v(17, 4, 16, C), ms0=f(3, 16 * 32, 128), ms1=f(3, 16 * 32, 128), mc=f(3, 6 * 24, 128), ml=v(3, 6, 16, C),
-        bfm=f(10, 32, C), bfe=f(3, 2 * 16, 128), fs0=f(3, 24 * 32, 128), fs3=f(3, 24 * 32, 128),
-        ge=f(3, 2 * 32, 128), tile=f(3, 48, 128), ts=f(3, 96, 128), tk=f(3, 64, 128),
+        pf=v(10, 4, 16, C), sm0=f(3, 17 * 32, 128), sm1=f(3, 17 * 32, 128), pre_m=f(8, 32, C), am=f(8, 32, C),
+        slm=f(3, 17 * 32, 128), sle=f(3, 5 * 16, 128), slb=v(8, 32, C), pml=v(4, 16, C), sc=f(3, 12 * 48, 128),
+        cb=v(3, 10, 32, C), gs=f(3, 8 * 48, 128), gb=v(3, 13, 32, C), bm=f(3, 9 * 32, 128),
+        mg=v(17, 4, 16, C), ms0=f(3, 17 * 32, 128), ms1=f(3, 17 * 32, 128), mc=f(3, 6 * 24, 128), ml=v(3, 6, 16, C),
+        bfm=f(10, 32, C), bfe=f(3, 2 * 16, 128), fs0=f(3, 25 * 32, 128), fs3=f(3, 25 * 32, 128),
+        ge=f(3, 2 * 32, 128), tile=f(3, 48, 128), ts=f(3, 96, 128), tk=f(3, 80, 128),
         c_buf=v(2, 48, C), k_buf=v(4, 16, C), r_slot=v(2, 3, 64, C), c_slot=v(2, 48, C), k_slot=v(4, 16, C),
         kp_buf=v(2, 16, 128), kp_slot=v(4, 16, 128),
         lr_buf=v(2, 96, C), lc_buf=v(2, 48, C), lk_buf=v(4, 16, C),
@@ -898,7 +898,7 @@
     vmem = pl.BlockSpec(memory_space=pltpu.VMEM)
     results = pl.pallas_call(
         functools.partial(kernel, nlat, nlon),
-        out_shape=(f(3, 16 * 64, 128), f(4, 16, C), v(21, 6, 16, C), v(*weight)),
+        out_shape=(f(3, 17 * 64, 128), f(4, 16, C), v(21, 6, 16, C), v(*weight)),
         in_specs=[hbm] * 5,
         out_specs=(vmem,) * 4,
         scratch_shapes=list(scratch.values()),
@@ -912,7 +912,7 @@
         out_shape=(shape, shape),
         in_specs=[vmem] * 4,
         out_specs=(hbm, hbm),
-        scratch_shapes=[v(*field), v(*field), f(3, 16 * 64, 128), f(3, 4 * 64, 128), pltpu.SemaphoreType.DMA((3,))],
+        scratch_shapes=[v(*field), v(*field), f(3, 17 * 64, 128), f(3, 5 * 64, 128), pltpu.SemaphoreType.DMA((3,))],
         compiler_params=pltpu.CompilerParams(vmem_limit_bytes=36 * 2**20),
     )(*results)
 

time: 45.9 us -> 45.9 us (level)
  no operation moved by 1% of the time
where the time goes in v3:
time: 45.9 us; the launch traced here: 45.8 us
  Pallas kernels  45 us (98%)
  between operations  0.8 us (2%)
    pallas_call x1, Pallas kernels, body(): pl.pallas_call(functools.partial(kernel, nlat, nlon), out_shape=(f(3, 17...  40 us
    pallas_call x1, Pallas kernels, body(): pl.pallas_call(functools.partial(last_kernel, nlat), out_shape=(shape, sh...  5.05 us

profile of v3, /device:TPU:1, one launch (start us, length us, event | category | flops | bytes accessed | tf_op | source)
XLA Modules:
  0.0 45.8 jit_solution(12675683254459558092)
XLA Ops:
  0.6 40.0 %shard_map.68 = (f32[3,1088,128]{2,1,0:T(8,128)S(1)}, f32[4,16,384]{2,1,0:T(8,128)S(1)}, bf16[21,6,16,384]{3,2,1,0:T(8,128)(2,1)S(1)}, bf16[3,3,384,384]{3,2,1,0:T(8,128)(2,1)S(1)}) custom-call(bf16[16,64,384]{2,1,0:T(8,128)(2,1)} %hid_hbm.1, bf16[16,64,384]{2,1,0:T(8,128)(2,1)} %cot_hbm.1, bf16[3,3,384,384]{3,2,1,0:T(8,128)(2,1)} %wf_hbm.1, ...), custom_call_target="tpu_custom_call" | custom-call | tf_op jit(solution)/shard_map/pallas_call | solution.py:899
  40.6 5.1 %shard_map.69 = (bf16[16,64,384]{2,1,0:T(8,128)(2,1)}, bf16[16,64,384]{2,1,0:T(8,128)(2,1)}) custom-call(f32[3,1088,128]{2,1,0:T(8,128)S(1)} %get-tuple-element.6.ns, f32[4,16,384]{2,1,0:T(8,128)S(1)} %get-tuple-element.7.ac, bf16[21,6,16,384]{3,2,1,0:T(8,128)(2,1)S(1)} %get-tuple-element.8.g_ext, bf16[3,3,384,384]{3,2,1,0:T(8,128)(2,1)S(1)} %get-tuple-element.9.wf), custom_call_target="tpu_custom_call" | custom-call | tf_op jit(solution)/shard_map/pallas_call | solution.py:910

commit v4 on v3

--- a/solution.py
+++ b/solution.py
@@ -573,10 +573,12 @@
         send(2, d, pk_buf.at[d - 4], pk_slot, 4)
     for d in (2, 3):
         send(2, d, pc_buf.at[d - 2], pc_slot, 2)
-    for d in (0, 1):
-        send(3, d, slb.at[pl.ds(6 * d, 2)], sr_slot, 0)
-    for d in (0, 1):
-        send(4, d, ctp.at[1 + 15 * d], ct_slot, 0)
+    for kind in (3, 4):
+        for d, k, to, target in ((0, far_d, far_slot, far), (1, near_d, near_slot, near)):
+            src, dst = (slb.at[pl.ds(6 * k, 2)], sr_slot) if kind == 3 else (ctp.at[1 + 15 * k], ct_slot)
+            copy = remote(kind, d, src, dst.at[to], to, target)
+            copy.start()
+            sends.append(copy)
     @pl.when(pole)
     def _():
         sl_buf[...] = row_get(slp, pole_row, 0, 64).astype(BF16)

time: 45.9 us -> 45.9 us (level)
  no operation moved by 1% of the time
where the time goes in v4:
time: 45.9 us; the launch traced here: 45.8 us
  Pallas kernels  45 us (98%)
  between operations  0.8 us (2%)
    pallas_call x1, Pallas kernels, body(): pl.pallas_call(functools.partial(kernel, nlat, nlon), out_shape=(f(3, 17...  40 us
    pallas_call x1, Pallas kernels, body(): pl.pallas_call(functools.partial(last_kernel, nlat), out_shape=(shape, sh...  5.05 us

profile of v4, /device:TPU:1, one launch (start us, length us, event | category | flops | bytes accessed | tf_op | source)
XLA Modules:
  0.0 45.8 jit_solution(6181077291989864877)
XLA Ops:
  0.6 40.0 %shard_map.68 = (f32[3,1088,128]{2,1,0:T(8,128)S(1)}, f32[4,16,384]{2,1,0:T(8,128)S(1)}, bf16[21,6,16,384]{3,2,1,0:T(8,128)(2,1)S(1)}, bf16[3,3,384,384]{3,2,1,0:T(8,128)(2,1)S(1)}) custom-call(bf16[16,64,384]{2,1,0:T(8,128)(2,1)} %hid_hbm.1, bf16[16,64,384]{2,1,0:T(8,128)(2,1)} %cot_hbm.1, bf16[3,3,384,384]{3,2,1,0:T(8,128)(2,1)} %wf_hbm.1, ...), custom_call_target="tpu_custom_call" | custom-call | tf_op jit(solution)/shard_map/pallas_call | solution.py:901
  40.6 5.1 %shard_map.69 = (bf16[16,64,384]{2,1,0:T(8,128)(2,1)}, bf16[16,64,384]{2,1,0:T(8,128)(2,1)}) custom-call(f32[3,1088,128]{2,1,0:T(8,128)S(1)} %get-tuple-element.6.ns, f32[4,16,384]{2,1,0:T(8,128)S(1)} %get-tuple-element.7.ac, bf16[21,6,16,384]{3,2,1,0:T(8,128)(2,1)S(1)} %get-tuple-element.8.g_ext, bf16[3,3,384,384]{3,2,1,0:T(8,128)(2,1)S(1)} %get-tuple-element.9.wf), custom_call_target="tpu_custom_call" | custom-call | tf_op jit(solution)/shard_map/pallas_call | solution.py:912
